TPU v7x, 256 devices: a whole 4x4x8 slice. The times are simulated.
256 devices in a mesh: row: 4 (over x), col: 16 (over y, z_lo), sample: 4 (over z_hi, core).
Axes of the slice: x: 4, y: 4, z: 8 (z_hi: 2, z_lo: 4; z = z_hi * 4 + z_lo), core: 2. Of those that a mesh axis runs over, the one named last changes fastest.
Arguments:
- pair: bfloat16 [2048, 2048, 128], P('row', ('col', 'sample')), may hold values from -6 to 6
- pair_gain: float32 [128], replicated, may hold values from 0.25 to 1.75
- pair_weight: bfloat16 [128, 16], replicated, may hold values from -0.5 to 0.5
- queries: bfloat16 [40, 16, 48, 2048], P('sample', 'col', None, 'row'), may hold values from -400 to 400
- keys: bfloat16 [40, 16, 48, 2048], P('sample', 'col', None, 'row'), may hold values from -5 to 5
- values: bfloat16 [40, 16, 48, 2048], P('sample', 'col', None, 'row'), may hold values from -6 to 6
- d_atoms: bfloat16 [40, 16, 48, 8192], P('sample', 'col', None, 'row'), may hold values from -768 to 768
- key_mask: int32 [2048], P('row'), may hold values 0 or 1
- atom_token: int32 [8192], P('row'), may hold values from 0 to 2047, as said below
Outputs:
- attn_out: bfloat16 [40, 16, 48, 2048], P('sample', 'col', None, 'row')
- d_query: bfloat16 [40, 16, 48, 2048], P('sample', 'col', None, 'row')
- d_pair: bfloat16 [2048, 2048, 128], P('row', ('col', 'sample'))
Inputs may be any that keep to these rules, and one draw needn't show every extreme that they name: `atom_token`: the atoms of the i-th aligned block of 2048 atoms name tokens of the i-th block of 512 tokens, the block's first and last token among them.
All inputs are finite; a program needn't handle non-finite values. No bound on the sum of `key_mask` on one device may be relied on, other than what follows from the above.
Results may differ from a plain program's by a relative error of at most 0.025.
Values may be sent and summed in bfloat16 or wider, within the bound.
No kernel may reach another device: no remote copies, remote signals or barrier semaphores. Data moves between devices by JAX's collectives and lax.ppermute only.
A program may use at most 128 MiB of HBM per device.

v0:
```python
import math

import jax
import jax.numpy as jnp
from jax import lax
from jax.sharding import PartitionSpec as P

EPS = 1e-05
HIGH = lax.Precision.HIGHEST


def normalize(pair_block, pair_gain):
    widened = pair_block.astype(jnp.float32)
    centred = widened - jnp.mean(widened, axis=-1, keepdims=True)
    inverse = lax.rsqrt(jnp.mean(centred * centred, axis=-1, keepdims=True) + EPS)
    hatted = centred * inverse
    return ((hatted * pair_gain).astype(jnp.bfloat16), hatted, inverse)


def norm_backward(d_normed, hatted, inverse, pair_gain):
    scaled = d_normed * pair_gain
    return inverse * (
        scaled
        - jnp.mean(scaled, axis=-1, keepdims=True)
        - hatted * jnp.mean(scaled * hatted, axis=-1, keepdims=True)
    )


def attend(query_cols, key_cols, value_cols, grad_cols, strip_bias, usable, scaling):
    contract = (((0,), (0,)), ((), ()))
    scores = (
        lax.dot_general(key_cols, query_cols, contract, preferred_element_type=jnp.float32)
        * scaling
    )
    scores = jnp.where(usable[:, None], scores + strip_bias.astype(jnp.float32), -1000000000.0)
    row_max = jnp.max(scores, axis=0, keepdims=True)
    exponent = jnp.exp(scores - row_max)
    chances = exponent / jnp.sum(exponent, axis=0, keepdims=True)
    weights = chances.astype(jnp.bfloat16)
    output = jnp.dot(value_cols, weights, preferred_element_type=jnp.float32).astype(jnp.bfloat16)
    d_chances = lax.dot_general(value_cols, grad_cols, contract, preferred_element_type=jnp.float32)
    centre = jnp.sum(
        grad_cols.astype(jnp.float32) * output.astype(jnp.float32), axis=0, keepdims=True
    )
    d_scores = chances * (d_chances - centre)
    d_weights = d_scores.astype(jnp.bfloat16)
    d_query = (jnp.dot(key_cols, d_weights, preferred_element_type=jnp.float32) * scaling).astype(
        jnp.bfloat16
    )
    return (output, d_query, d_scores)


def local(pair, pair_gain, pair_weight, queries, keys, values, d_atoms, key_mask, atom_token):
    normed, hatted, inverse = normalize(pair, pair_gain)
    tile_bias = jnp.einsum(
        "rwc,ch->hwr", normed, pair_weight, preferred_element_type=jnp.float32
    ).astype(jnp.bfloat16)
    widened = lax.all_gather(tile_bias, "sample", axis=1, tiled=True)
    strip_bias = lax.all_to_all(widened, "col", split_axis=0, concat_axis=1, tiled=True)
    key_all, value_all, mask_all = (
        lax.all_gather(keys, "row", axis=3, tiled=True),
        lax.all_gather(values, "row", axis=3, tiled=True),
        lax.all_gather(key_mask, "row", axis=0, tiled=True),
    )
    usable = mask_all > 0
    strip_rows = queries.shape[3]
    offset = lax.axis_index("row") * strip_rows
    onehot = (
        atom_token[:, None] - offset == jnp.arange(strip_rows, dtype=jnp.int32)[None, :]
    ).astype(jnp.bfloat16)
    grad_out = jnp.einsum(
        "shda,at->shdt", d_atoms, onehot, preferred_element_type=jnp.float32
    ).astype(jnp.bfloat16)
    scaling = 1.0 / math.sqrt(queries.shape[2])

    def per_sample(running, inputs):
        query_cols, key_cols, value_cols, grad_cols = inputs
        output, d_query, d_scores = jax.vmap(
            lambda qc, kc, vc, gc, bc: attend(qc, kc, vc, gc, bc, usable, scaling)
        )(query_cols, key_cols, value_cols, grad_cols, strip_bias)
        return (running + d_scores, (output, d_query))

    d_bias, (outputs, d_queries) = lax.scan(
        per_sample,
        jnp.zeros(strip_bias.shape, jnp.float32),
        (queries, key_all, value_all, grad_out),
    )
    by_heads = lax.all_to_all(d_bias, "col", split_axis=1, concat_axis=0, tiled=True)
    tile_grad = lax.psum_scatter(by_heads, "sample", scatter_dimension=1, tiled=True)
    d_normed = jnp.einsum("hwr,ch->rwc", tile_grad, pair_weight.astype(jnp.float32), precision=HIGH)
    d_pair = norm_backward(d_normed, hatted, inverse, pair_gain).astype(jnp.bfloat16)
    return (outputs, d_queries, d_pair)


def solution(mesh):
    placed = (
        P("row", ("col", "sample"), None),
        P(),
        P(),
        P("sample", "col", None, "row"),
        P("sample", "col", None, "row"),
        P("sample", "col", None, "row"),
        P("sample", "col", None, "row"),
        P("row"),
        P("row"),
    )
    return jax.shard_map(
        local,
        mesh=mesh,
        in_specs=placed,
        out_specs=(
            P("sample", "col", None, "row"),
            P("sample", "col", None, "row"),
            P("row", ("col", "sample"), None),
        ),
        check_vma=False,
    )
```

profile of v0, /device:TPU:8, one launch (start us, length us, event | category | flops | bytes accessed | tf_op | source)
XLA Modules:
  0.0 471.2 jit_solution(18439452161478279001)
XLA Ops:
  7.2 7.7 %copy.23 = bf16[512,32,128]{0,2,1:T(8,128)(2,1)} copy(bf16[512,32,128]{2,1,0:T(8,128)(2,1)} %param.11) | data formatting | bytes 8388608 | tf_op args[0]
  14.9 3.1 convert_reduce_fusion
  18.3 1.3 fusion.49
  19.7 2.2 fusion.68
  22.0 0.7 all-gather.5.cloned.1.call-update
  22.7 45.5 %all-gather.7.cloned.1.call-done = bf16[16,128,512]{2,0,1:T(8,128)(2,1)} async-done(((bf16[16,32,512]{2,0,1:T(8,128)(2,1)}), bf16[16,128,512]{2,0,1:T(8,128)(2,1)}) %all-gather.7.cloned.1.call-update) | async-done | bytes 2097168 | tf_op jit(solution)/shard_map/all_gather | solution.py:58
  68.2 4.1 copy.25
  72.3 5.0 %all-to-all-start = ((bf16[16,128,512]{2,1,0:T(8,128)(2,1)}), bf16[16,128,512]{2,1,0:T(8,128)(2,1)}, u32[]{:S(2)}, u32[]{:S(2)}) async-start(bf16[16,128,512]{2,1,0:T(8,128)(2,1)} %copy.25), calls=%async_computation | async-start | bytes 4194304 | tf_op jit(solution)/shard_map/all_to_all | solution.py:59
  77.4 0.7 all-gather.9.cloned.1.call-update
  78.1 11.2 %all-gather = s32[4,1,512]{2,1,0:T(1,128)S(1)} all-gather(s32[1,1,512]{2,1,0:T(1,128)S(1)} %bitcast.105), channel_id=1, replica_groups=mesh['row'=4,'col'=16,'sample'=4] {'row'}, dimensions={0}, use_global_device_ids=true | all-gather | bytes 10240 | tf_op jit(solution)/shard_map/all_gather | solution.py:63
  89.4 1.4 fusion.71
  90.8 7.9 %all-gather.5.cloned.1.call-done = bf16[10,1,48,2048]{3,2,1,0:T(8,128)(2,1)} async-done(((bf16[10,1,48,512]{3,2,1,0:T(8,128)(2,1)}), bf16[10,1,48,2048]{3,2,1,0:T(8,128)(2,1)}) %all-gather.5.cloned.1.call-update) | async-done | bytes 1966096 | tf_op jit(solution)/shard_map/all_gather | solution.py:61
  98.7 34.0 %all-gather.9.cloned.1.call-done = bf16[10,1,48,2048]{3,2,1,0:T(8,128)(2,1)} async-done(((bf16[10,1,48,512]{3,2,1,0:T(8,128)(2,1)}), bf16[10,1,48,2048]{3,2,1,0:T(8,128)(2,1)}) %all-gather.9.cloned.1.call-update) | async-done | bytes 1966096 | tf_op jit(solution)/shard_map/all_gather | solution.py:62
  132.8 119.2 %while.15 = (s32[]{:T(128)}, f32[1,2048,512]{2,1,0:T(8,128)}, bf16[10,1,48,512]{3,2,1,0:T(8,128)(2,1)}, bf16[10,1,48,512]{3,2,1,0:T(8,128)(2,1)}, pred[2048]{0:T...) while((s32[]{:T(128)}, f32[1,2048,512]{2,1,0:T(8,128)}, ...), condition=%wide.region_6.7_spmd.clone, body=%wide.region_2.6_spmd.clone.sunk | while | flops 420649472 | bytes 66167488 | solution.py:83
  132.8 2.7 fusion.89
  136.1 1.9 multiply_reduce_fusion.2
  138.7 3.7 bitcast_add_fusion.2
  142.4 2.3 fusion.91
  144.7 2.7 fusion.89
  147.4 0.6 fusion.90
  148.0 1.9 multiply_reduce_fusion.2
  150.6 3.7 bitcast_add_fusion.2
  154.3 2.3 fusion.91
  156.6 2.7 fusion.89
  160.0 1.9 multiply_reduce_fusion.2
  162.5 3.7 bitcast_add_fusion.2
  166.2 2.3 fusion.91
  168.5 2.7 fusion.89
  171.2 0.6 fusion.90
  171.9 1.9 multiply_reduce_fusion.2
  174.4 3.7 bitcast_add_fusion.2
  178.2 2.3 fusion.91
  180.4 2.7 fusion.89
  183.2 0.6 fusion.90
  183.8 1.9 multiply_reduce_fusion.2
  186.3 3.7 bitcast_add_fusion.2
  190.1 2.3 fusion.91
  192.3 2.7 fusion.89
  195.7 1.9 multiply_reduce_fusion.2
  198.2 3.7 bitcast_add_fusion.2
  202.0 2.3 fusion.91
  204.3 2.7 fusion.89
  207.6 1.9 multiply_reduce_fusion.2
  210.2 3.7 bitcast_add_fusion.2
  213.9 2.3 fusion.91
  216.2 2.7 fusion.89
  219.5 1.9 multiply_reduce_fusion.2
  222.1 3.7 bitcast_add_fusion.2
  225.8 2.3 fusion.91
  228.1 2.7 fusion.89
  231.5 1.9 multiply_reduce_fusion.2
  234.0 3.7 bitcast_add_fusion.2
  237.7 2.3 fusion.91
  240.0 2.7 fusion.89
  243.4 1.9 multiply_reduce_fusion.2
  245.9 3.7 bitcast_add_fusion.2
  249.7 2.3 fusion.91
  251.9 7.0 %copy.27 = f32[1,2048,512]{2,0,1:T(1,128)S(1)} copy(f32[1,2048,512]{2,1,0:T(8,128)} %get-tuple-element.59) | data formatting | bytes 8388608 | tf_op jit(solution)/shard_map/while | solution.py:83
  259.0 100.0 %all_to_all.24 = f32[1,2048,512]{2,0,1:T(1,128)S(1)} all-to-all(f32[1,2048,512]{2,0,1:T(1,128)S(1)} %copy.27), channel_id=1, replica_groups=mesh['row'=4,'col'=16,'sample'=4] {'col'}, dimensions={1} | all-to-all | bytes 8388608 | tf_op jit(solution)/shard_map/all_to_all | solution.py:88
  359.4 4.4 copy.28
  363.9 79.7 %reduce-scatter.2.cloned.1.call-done = f32[16,32,512]{2,0,1:T(8,128)} async-done(((f32[16,128,512]{2,0,1:T(8,128)}), f32[16,32,512]{2,0,1:T(8,128)}) %reduce-scatter.2.cloned.1.call-update) | async-done | bytes 1048592 | tf_op jit(solution)/shard_map/reduce_scatter | solution.py:89
  443.5 9.0 %bitcast_reduce_fusion = (f32[512,32]{0,1:T(8,128)S(1)}, f32[512,32]{0,1:T(8,128)S(1)}, f32[32,512,128]{1,2,0:T(8,128)S(1)}) fusion(f32[128]{0:T(128)S(1)} %copy-done.8, f32[512,32]{0,1:T(8,128)S(1)} %add_rsqrt_fusion, f32[512,32]{0,1:T(8,128)S(1)} %broadcast_multiply_fusion.2, bf16[512,32,128]{0,2,1:T(8,128)(2,1)} %copy.23, ...), kind=kOutput, calls=%fused_computation.48 | convolution fusion | flops 417300480 | bytes 13898240 | tf_op jit(solution)/shard_map/hwr,ch->rwc/dot_general | solution.py:90
  452.5 4.3 fusion.48
  456.8 7.8 %copy.29 = bf16[512,32,128]{2,1,0:T(8,128)(2,1)} copy(bf16[512,32,128]{0,2,1:T(8,128)(2,1)} %fusion.48) | data formatting | bytes 8388608
  (90 shorter events, 11.9 us)
Async XLA Ops:
  7.2 82.3 %copy-start = (bf16[10,1,48,2048]{3,2,1,0:T(8,128)(2,1)S(1)}, bf16[10,1,48,2048]{3,2,1,0:T(8,128)(2,1)}, u32[]{:S(2)}) copy-start(bf16[10,1,48,2048]{3,2,1,0:T(8,128)(2,1)} %param.17) | copy-start | bytes 5898244
  7.2 61.0 %all-gather.7.cloned.1.call-start = ((), (), s32[]{:S(2)}) async-start(), calls=%async_computation.4 | async-start | bytes 2621440 | tf_op jit(solution)/shard_map/all_gather | solution.py:58
  14.9 3.4 copy-start.2
  14.9 4.8 %copy-start.8 = (f32[128]{0:T(128)S(1)}, f32[128]{0:T(128)}, u32[]{:S(2)}) copy-start(f32[128]{0:T(128)} %param.12) | copy-start | bytes 1540
  14.9 4.8 %copy-start.9 = (bf16[128,16]{0,1:T(8,128)(2,1)S(1)}, bf16[128,16]{0,1:T(8,128)(2,1)}, u32[]{:S(2)}) copy-start(bf16[128,16]{0,1:T(8,128)(2,1)} %param.13) | copy-start | bytes 12292
  21.9 76.8 %all-gather.5.cloned.1.call-start = ((), (), s32[]{:S(2)}) async-start(), calls=%async_computation.3 | async-start | bytes 2457600 | tf_op jit(solution)/shard_map/all_gather | solution.py:61
  22.7 55.5 %copy-start.7 = (s32[512]{0:T(512)S(1)}, s32[512]{0:T(512)}, u32[]{:S(2)}) copy-start(s32[512]{0:T(512)} %param.18) | copy-start | bytes 6148
  22.7 66.7 %copy-start.6 = (s32[2048]{0:T(1024)S(1)}, s32[2048]{0:T(1024)}, u32[]{:S(2)}) copy-start(s32[2048]{0:T(1024)} %param.19) | copy-start | bytes 24580
  72.3 60.5 %all-to-all-start = ((bf16[16,128,512]{2,1,0:T(8,128)(2,1)}), bf16[16,128,512]{2,1,0:T(8,128)(2,1)}, u32[]{:S(2)}, u32[]{:S(2)}) async-start(bf16[16,128,512]{2,1,0:T(8,128)(2,1)} %copy.25), calls=%async_computation | async-start | bytes 4194304 | tf_op jit(solution)/shard_map/all_to_all | solution.py:59
  77.3 55.4 %all-gather.9.cloned.1.call-start = ((), (), s32[]{:S(2)}) async-start(), calls=%async_computation.5 | async-start | bytes 2457600 | tf_op jit(solution)/shard_map/all_gather | solution.py:62
  78.0 365.5 %reduce-scatter.2.cloned.1.call-start = ((), (), s32[]{:S(2)}) async-start(), calls=%async_computation.6 | async-start | bytes 5242880 | tf_op jit(solution)/shard_map/reduce_scatter | solution.py:89
  136.1 2.5 copy-start.4
  142.4 2.3 copy-start.5
  148.0 2.5 copy-start.4
  154.3 2.3 copy-start.5
  160.0 2.5 copy-start.4
  166.2 2.3 copy-start.5
  171.9 2.5 copy-start.4
  178.1 2.3 copy-start.5
  183.8 2.5 copy-start.4
  190.1 2.3 copy-start.5
  195.7 2.5 copy-start.4
  202.0 2.3 copy-start.5
  207.6 2.5 copy-start.4
  213.9 2.3 copy-start.5
  219.5 2.5 copy-start.4
  225.8 2.3 copy-start.5
  231.4 2.5 copy-start.4
  237.7 2.3 copy-start.5
  243.4 2.5 copy-start.4
  249.6 2.3 copy-start.5
  443.5 9.0 %copy-start.3 = (bf16[512,32,128]{0,2,1:T(8,128)(2,1)S(1)}, bf16[512,32,128]{0,2,1:T(8,128)(2,1)}, u32[]{:S(2)}) copy-start(bf16[512,32,128]{0,2,1:T(8,128)(2,1)} %copy.23) | copy-start | bytes 12582916
  452.5 12.1 %copy-start.1 = (bf16[10,1,48,2048]{3,2,1,0:T(8,128)(2,1)S(1)}, bf16[10,1,48,2048]{3,2,1,0:T(8,128)(2,1)}, u32[]{:S(2)}) copy-start(bf16[10,1,48,2048]{3,2,1,0:T(8,128)(2,1)} %param.17) | copy-start | bytes 5898244
Sparse Core Ops, SparseCore 0:
  22.0 46.1 all-gather.6
  70.0 28.6 all-gather.4
  100.5 32.1 all-gather.8
  364.0 79.4 reduce-scatter.1
where the time goes:
time: 474 us; the launch traced here: 471 us
  waiting for transfers between devices  169 us (36%)
  matrix products  119 us (25%)
  blocking collectives  111 us (23%)
  local copies, waits for them, and re-layouts  38.3 us (8%)
  other arithmetic  15.1 us (3%)
  between operations  14 us (3%)
  starting transfers between devices  5.19 us (1%)
    all_to_all x1, blocking collectives, local(): lax.all_to_all(d_bias, 'col', split_axis=1, concat_axis=0, tiled=True)  100 us
    reduce_scatter x1, waiting for transfers between devices, local(): lax.psum_scatter(by_heads, 'sample', scatter_dimension=1, tiled=True)  79.7 us
    all_gather x1, waiting for transfers between devices, local(): widened = lax.all_gather(tile_bias, 'sample', axis=1, tiled=True)  45.5 us
    dot_general x10, matrix products, attend(): lax.dot_general(value_cols, grad_cols, contract, preferred_element_type=j...  37.3 us
    all_gather x1, waiting for transfers between devices, local(): lax.all_gather(values, 'row', axis=3, tiled=True)  34 us
    dot_general x10, matrix products, attend(): lax.dot_general(key_cols, query_cols, contract, preferred_element_type=jn...  27.2 us
    dot_general x10, matrix products, attend(): jnp.dot(key_cols, d_weights, preferred_element_type=jnp.float32) * scaling  22.6 us
    dot_general x10, matrix products, attend(): jnp.dot(value_cols, weights, preferred_element_type=jnp.float32)  19 us
  transfers between devices with their start and end apart: 5, of which 4 were waited for; matrix products, arithmetic and copies ran while one was open for 1% of the time, Pallas kernels for 0%

commit v1 on v0

v1 whole, which is shorter than its diff:
```python
import functools
import math

import jax
import jax.numpy as jnp
from jax import lax
from jax.experimental import pallas as pl
from jax.experimental.pallas import tpu as pltpu
from jax.sharding import Mesh, PartitionSpec as P

EPS = 1e-05
HIGH = lax.Precision.HIGHEST
F32, BF16 = jnp.float32, jnp.bfloat16
LOG2E = 1.4426950408889634
NEG = -1e9
TN = (((0,), (0,)), ((), ()))


def attn_kernel(JT, core_ref, mine_ref, other_ref, q_ref, k_ref, v_ref, m_ref, g_ref,
                o_ref, dq_ref, keep_ref, send_ref,
                bias_s, acc_s, s_s, e_s, kt_s, vt_s, kc_s, vc_s):
    step = pl.program_id(0)
    steps = pl.num_programs(0)
    n_i = q_ref.shape[-1]
    dh = q_ref.shape[-2]
    n_j = bias_s.shape[0]
    rows = k_ref.shape[0]
    per = n_j // rows
    core = core_ref[0]
    blocks = mine_ref.shape[0]
    bj = mine_ref.shape[1]
    scaling = 1.0 / math.sqrt(dh)

    @pl.when(step == 0)
    def _():
        for src, par in ((mine_ref, core), (other_ref, 1 - core)):
            @pl.loop(0, blocks)
            def _(b):
                at = pl.multiple_of((b * 2 + par) * bj, bj)
                bias_s[pl.ds(at, bj), :] = src[b].astype(F32) * LOG2E
        mcol = jnp.concatenate([m_ref[r, 0, :8, :].astype(F32) for r in range(rows)], 1).T
        for t in range(0, n_j, 256):
            m = mcol[t:t + 256, 0:1]
            bias_s[t:t + 256, :] = jnp.where(m > 0, bias_s[t:t + 256, :], NEG)
        acc_s[...] = jnp.zeros_like(acc_s)


    for r in range(rows):
        sl = slice(r * per, (r + 1) * per)
        k = k_ref[r, 0]
        v = v_ref[r, 0]
        kz = k * m_ref[r, 0]
        kt_s[sl, :] = jnp.concatenate([kz, kz], 0).T
        one = jnp.ones((16, per), BF16)
        vt_s[sl, :] = jnp.concatenate([v, v, one], 0).T
        kc_s[:, sl] = k
        vc_s[:, sl] = jnp.concatenate([v, one], 0)

    q = q_ref[0].astype(F32) * (scaling * LOG2E)
    qh = q.astype(BF16)
    ql = (q - qh.astype(F32)).astype(BF16)
    q2 = jnp.concatenate([qh, ql], 0)
    IH = 256
    for h in range(n_i // IH):
        il = slice(h * IH, (h + 1) * IH)
        m = None
        for t in range(0, n_j, JT):
            s = jnp.dot(kt_s[t:t + JT, :], q2[:, il], preferred_element_type=F32) + bias_s[t:t + JT, il]
            s_s[t:t + JT, :] = s
            mt = jnp.max(s.reshape(JT // 8, 8, IH), axis=0)
            m = mt if m is None else jnp.maximum(m, mt)
        m = jnp.max(m, axis=0, keepdims=True)
        o = None
        for t in range(0, n_j, JT):
            e = jnp.exp2(s_s[t:t + JT, :] - m).astype(BF16)
            e_s[t:t + JT, :] = e
            ot = jnp.dot(vc_s[:, t:t + JT], e, preferred_element_type=F32)
            o = ot if o is None else o + ot
        inv = 1.0 / o[dh:dh + 1, :]
        o = o[:dh] * inv
        o_ref[0, :, il] = o.astype(BF16)
        g = g_ref[0, :, il].astype(F32)
        centre = jnp.sum(g * o, axis=0, keepdims=True)
        g = g * inv
        c = -centre * inv
        gh = g.astype(BF16)
        gl = (g - gh.astype(F32)).astype(BF16)
        ch = c.astype(BF16).astype(F32)
        cl = c - ch
        row = lax.broadcasted_iota(jnp.int32, (16, IH), 0)
        cb = jnp.where(row == 0, ch, jnp.where(row == 1, cl, 0.0)).astype(BF16)
        g2 = jnp.concatenate([gh, gl, cb], 0)
        dq = None
        for t in range(0, n_j, JT):
            x = jnp.dot(vt_s[t:t + JT, :], g2, preferred_element_type=F32)
            ds = e_s[t:t + JT, :].astype(F32) * x
            acc_s[t:t + JT, il] += ds
            dt = jnp.dot(kc_s[:, t:t + JT], ds.astype(BF16), preferred_element_type=F32)
            dq = dt if dq is None else dq + dt
        dq_ref[0, :, il] = (dq * scaling).astype(BF16)

    @pl.when(step == steps - 1)
    def _():
        for dst, par in ((keep_ref, core), (send_ref, 1 - core)):
            @pl.loop(0, blocks)
            def _(b):
                at = pl.multiple_of((b * 2 + par) * bj, bj)
                dst[b] = acc_s[pl.ds(at, bj), :].astype(BF16)


def attention(core, mine, other, q, kv, g, JT=1024):
    S, dh, I = q.shape
    R, per = kv.shape[0], kv.shape[3]
    J = R * per
    full = lambda a: pl.BlockSpec(a.shape, lambda s: (0,) * a.ndim)
    qspec = pl.BlockSpec((1, dh, I), lambda s: (s, 0, 0))
    kspec = pl.BlockSpec((R, 1, dh, per), lambda s: (0, s, 0, 0))
    vspec = pl.BlockSpec((R, 1, dh, per), lambda s: (0, s + S, 0, 0))
    mspec = pl.BlockSpec((R, 1, dh, per), lambda s: (0, 2 * S, 0, 0))
    IH = 256
    return pl.pallas_call(
        functools.partial(attn_kernel, JT),
        grid=(S,),
        in_specs=[pl.BlockSpec(memory_space=pltpu.SMEM), full(mine), full(other),
                  qspec, kspec, vspec, mspec, qspec],
        out_specs=[qspec, qspec, full(mine), full(other)],
        out_shape=[jax.ShapeDtypeStruct(q.shape, BF16), jax.ShapeDtypeStruct(q.shape, BF16),
                   jax.ShapeDtypeStruct(mine.shape, BF16), jax.ShapeDtypeStruct(other.shape, BF16)],
        scratch_shapes=[pltpu.VMEM((J, I), F32), pltpu.VMEM((J, I), F32),
                        pltpu.VMEM((J, IH), F32), pltpu.VMEM((J, IH), BF16),
                        pltpu.VMEM((J, 2 * dh), BF16), pltpu.VMEM((J, 2 * dh + 16), BF16),
                        pltpu.VMEM((dh, J), BF16), pltpu.VMEM((dh + 16, J), BF16)],
        compiler_params=pltpu.CompilerParams(vmem_limit_bytes=48 * 1024 * 1024),
        cost_estimate=pl.CostEstimate(flops=8 * S * J * I * dh, bytes_accessed=12 * 1024 * 1024, transcendentals=S * I * J),
        name="attend",
    )(core, mine, other, q, kv, kv, kv, g)


def normalize(pair_block, pair_gain):
    widened = pair_block.astype(F32)
    centred = widened - jnp.mean(widened, axis=-1, keepdims=True)
    inverse = lax.rsqrt(jnp.mean(centred * centred, axis=-1, keepdims=True) + EPS)
    hatted = centred * inverse
    return ((hatted * pair_gain).astype(BF16), hatted, inverse)


def norm_backward(d_normed, hatted, inverse, pair_gain):
    scaled = d_normed * pair_gain
    return inverse * (
        scaled
        - jnp.mean(scaled, axis=-1, keepdims=True)
        - hatted * jnp.mean(scaled * hatted, axis=-1, keepdims=True)
    )


def local(pair, pair_gain, pair_weight, queries, keys, values, d_atoms, key_mask, atom_token):
    samples, _, dh, strip = queries.shape
    flags = jnp.broadcast_to(key_mask.astype(BF16), (1, dh, strip))
    kv = lax.all_gather(jnp.concatenate([keys[:, 0], values[:, 0], flags], 0), "row")

    normed, hatted, inverse = normalize(pair, pair_gain)
    tile_bias = jnp.einsum(
        "rwc,ch->hwr", normed, pair_weight, preferred_element_type=F32
    ).astype(BF16)
    heads, width, _ = tile_bias.shape
    out = jnp.broadcast_to(tile_bias[:, None], (heads, 2, width, strip)).reshape(2 * heads, width, strip)
    mine = lax.all_to_all(out, ("col", "zhi"), 0, 0, tiled=True)
    other = lax.ppermute(mine, "core", [(0, 1), (1, 0)])

    offset = lax.axis_index("row") * strip
    onehot = (
        atom_token[:, None] - offset == jnp.arange(strip, dtype=jnp.int32)[None, :]
    ).astype(BF16)
    grad_out = jnp.einsum(
        "sda,at->sdt", d_atoms[:, 0], onehot, preferred_element_type=F32
    ).astype(BF16)

    core = lax.axis_index("core").astype(jnp.int32).reshape(1)
    o, dq, keep, send = attention(core, mine, other, queries[:, 0], kv, grad_out)

    got = lax.ppermute(send, "core", [(0, 1), (1, 0)])
    chip = (keep.astype(F32) + got.astype(F32)).astype(BF16)
    parts = lax.all_to_all(chip, ("col", "zhi"), 0, 0, tiled=True)
    tile_grad = jnp.sum(parts.reshape(heads, 2, width, strip).astype(F32), axis=1)
    d_normed = jnp.einsum("hwr,ch->rwc", tile_grad, pair_weight.astype(F32), precision=HIGH)
    d_pair = norm_backward(d_normed, hatted, inverse, pair_gain).astype(BF16)
    return (o[:, None], dq[:, None], d_pair)


def solution(mesh):
    fine = Mesh(mesh.devices.reshape(4, 16, 2, 2), ("row", "col", "zhi", "core"))
    sample = ("zhi", "core")
    tokens = P(sample, "col", None, "row")
    tile = P("row", ("col", "zhi", "core"), None)
    return jax.shard_map(
        local,
        mesh=fine,
        in_specs=(tile, P(), P(), tokens, tokens, tokens, tokens, P("row"), P("row")),
        out_specs=(tokens, tokens, tile),
        check_vma=False,
    )
```

time: 474 us -> 172 us (0.36)
  waiting for transfers between devices: 169 us -> 3.15 us
  matrix products: 119 us -> 9.86 us
  Pallas kernels: 0 us -> 39.5 us
  blocking collectives: 111 us -> 73.1 us
  local copies, waits for them, and re-layouts: 38.3 us -> 16.8 us
  starting transfers between devices: 5.19 us -> 0.15 us
    dot_general x43 -> x3, matrix products: 119 us -> 9.86 us  [the longest x1 6.32 us: local(): jnp.einsum('hwr,ch->rwc', tile_grad, pair_weight.astype(F32), precision=H...]
    all_gather x3 -> x1, waiting for transfers between devices: 87.4 us -> 0.01 us  [local(): lax.all_gather(jnp.concatenate([keys[:, 0], values[:, 0], flags], 0), 'row')]
    reduce_scatter x1 -> x0, waiting for transfers between devices: 79.7 us -> none  [local(): lax.psum_scatter(by_heads, 'sample', scatter_dimension=1, tiled=True)]
    pallas_call x0 -> x1, Pallas kernels: none -> 39.5 us  [attention(): pl.pallas_call(functools.partial(attn_kernel, JT), grid=(S,), in_specs=[p...]
    all_to_all x1 -> x2, blocking collectives: 100 us -> 73.1 us  [the longest x1 39.5 us: local(): mine = lax.all_to_all(out, ('col', 'zhi'), 0, 0, tiled=True)]
    all_gather x1 -> x0, blocking collectives: 11.2 us -> none  [local(): lax.all_gather(key_mask, 'row', axis=0, tiled=True)]
    while x41 -> x0, local copies, waits for them, and re-layouts: 7.12 us -> none  [the longest x1 7.02 us: local(): lax.scan(per_sample, jnp.zeros(strip_bias.shape, jnp.float32), (queries,...]
    dynamic_update_slice x10 -> x0, local copies, waits for them, and re-layouts: 6.29 us -> none  [local(): lax.scan(per_sample, jnp.zeros(strip_bias.shape, jnp.float32), (queries,...]
  transfers between devices with their start and end apart: 5 -> 3, of which waited for: 4 -> 2; matrix products, arithmetic and copies ran while one was open for 1% -> 11% of each run, Pallas kernels for 0% -> 0%
where the time goes in v1:
time: 172 us
  blocking collectives  73.1 us (42%)
  Pallas kernels  39.5 us (23%)
  local copies, waits for them, and re-layouts  16.8 us (10%)
  other arithmetic  14.7 us (9%)
  between operations  14.2 us (8%)
  matrix products  9.86 us (6%)
  waiting for transfers between devices  3.15 us (2%)
    pallas_call x1, Pallas kernels, attention(): pl.pallas_call(functools.partial(attn_kernel, JT), grid=(S,), in_specs=[p...  39.5 us
    all_to_all x1, blocking collectives, local(): mine = lax.all_to_all(out, ('col', 'zhi'), 0, 0, tiled=True)  39.5 us
    all_to_all x1, blocking collectives, local(): parts = lax.all_to_all(chip, ('col', 'zhi'), 0, 0, tiled=True)  33.6 us
    unnamed x26, local copies, waits for them, and re-layouts  16.4 us
    dot_general x1, matrix products, local(): jnp.einsum('hwr,ch->rwc', tile_grad, pair_weight.astype(F32), precision=H...  6.32 us
    convert_element_type x1, other arithmetic, local(): d_pair = norm_backward(d_normed, hatted, inverse, pair_gain).astype(BF16)  4.29 us
    reduce_sum x1, other arithmetic, normalize(): jnp.mean(centred * centred, axis=-1, keepdims=True) + EPS  3.55 us
  transfers between devices with their start and end apart: 3, of which 2 were waited for; matrix products, arithmetic and copies ran while one was open for 11% of the time, Pallas kernels for 0%

profile of v1, /device:TPU:8, one launch (start us, length us, event | category | flops | bytes accessed | tf_op | source)
XLA Modules:
  0.0 171.5 jit_solution(1711186257687455389)
XLA Ops:
  7.2 0.0 copy-start
  7.2 0.0 all-gather.3.cloned.1.call-start
  7.2 0.8 convert_element_type.44
  8.1 2.3 %pad_maximum_fusion = bf16[21,48,512]{2,1,0:T(8,128)(2,1)} fusion(bf16[1,48,512]{2,1,0:T(8,128)(2,1)S(1)} %broadcast_in_dim.9, bf16[10,48,512]{2,1,0:T(8,128)(2,1)} %bitcast.48, bf16[10,48,512]{2,1,0:T(8,128)(2,1)} %bitcast.49), kind=kLoop, calls=%fused_computation.32 | loop fusion | flops 1032192 | bytes 2064384 | tf_op jit(solution)/shard_map/concatenate | solution.py:159
  10.4 0.0 all-gather.3.cloned.1.call-update
  10.4 0.0 copy-start.10
  10.4 0.0 copy-start.11
  10.4 7.5 %copy.18 = bf16[512,32,128]{0,2,1:T(8,128)(2,1)} copy(bf16[512,32,128]{2,1,0:T(8,128)(2,1)} %param.9) | data formatting | bytes 8388608 | tf_op args[0]
  17.9 0.0 copy-start.3
  17.9 3.1 %convert_reduce_fusion = f32[512,32]{0,1:T(8,128)S(1)} fusion(bf16[512,32,128]{0,2,1:T(8,128)(2,1)} %copy.18), kind=kLoop, calls=%fused_computation.1 | loop fusion | flops 4177920 | bytes 4259840 | tf_op jit(solution)/shard_map/reduce_sum | solution.py:141
  21.0 0.0 copy-start.5
  21.0 0.0 copy-start.9
  21.1 3.6 %fusion.10 = f32[512,32]{0,1:T(8,128)S(1)} fusion(bf16[512,32,128]{0,2,1:T(8,128)(2,1)} %copy.18, f32[512,32]{0,1:T(8,128)S(1)} %broadcast_multiply_fusion.2), kind=kLoop, calls=%fused_computation.12 | loop fusion | flops 8372224 | bytes 4325376 | tf_op jit(solution)/shard_map/reduce_sum | solution.py:142
  24.6 0.0 copy-done.10
  24.7 0.0 copy-done.11
  24.7 0.0 copy-done.3
  24.7 0.0 copy-start.7
  24.7 1.4 fusion.29
  26.1 0.0 copy-start.1
  26.1 0.3 copy.20
  26.4 0.1 broadcast_in_dim.8
  26.5 39.5 %all_to_all.10.mine_ref = bf16[32,32,512]{2,1,0:T(8,128)(2,1)S(1)} all-to-all(bf16[32,32,512]{2,1,0:T(8,128)(2,1)S(1)} %bitcast.47), channel_id=1, replica_groups=mesh['row'=4,'col'=16,'zhi'=2,'core'=2] {'col','zhi'}, dimensions={0} | all-to-all | bytes 2097152 | tf_op jit(solution)/shard_map/all_to_all | solution.py:167
  66.0 0.0 copy-done.5
  66.0 0.0 collective-permute-start
  66.0 0.0 copy-done.7
  66.0 0.0 copy-done.9
  66.0 0.0 copy-done
  66.0 2.2 %fusion.32.g_ref = bf16[10,48,512]{2,1,0:T(8,128)(2,1)} fusion(bf16[10,1,48,2048]{3,2,1,0:T(8,128)(2,1)S(1)} %copy-done, s32[2048]{0:T(1024)S(1)} %broadcast_subtract_fusion), kind=kOutput, calls=%fused_computation.29 | convolution fusion | flops 1007927296 | bytes 2465792 | tf_op jit(solution)/shard_map/sda,at->sdt/dot_general | solution.py:174
  68.2 0.6 collective-permute-done.other_ref
  68.8 0.0 all-gather.3.cloned.1.call-done
  68.8 0.0 copy-done.1
  68.8 0.0 copy-start.2
  68.8 1.0 copy-done.2
  69.8 0.0 copy-start.4
  69.8 0.0 copy-start.6
  69.8 0.0 copy-start.8
  69.8 39.5 %attend.1 = (bf16[10,48,512]{2,1,0:T(8,128)(2,1)}, bf16[10,48,512]{2,1,0:T(8,128)(2,1)}, bf16[32,32,512]{2,1,0:T(8,128)(2,1)S(1)}, bf16[32,32,512]{2,1,0:T(8,128)(2,1)S(1)}) custom-call(s32[1]{0:T(128)} %bitcast.core_ref, bf16[32,32,512]{2,1,0:T(8,128)(2,1)S(1)} %all_to_all.10.mine_ref, bf16[32,32,512]{2,1,0:T(8,128)(2,1)} %collective-permute-done.other_ref, ...), custom_call_target="tpu_custom_call" | custom-call | flops 4026531840 | bytes 12582912 | tf_op jit(solution)/shard_map/attend/pallas_call | solution.py:121
  109.4 0.1 collective-permute-start.1
  109.5 2.5 %collective-permute-done.1 = bf16[32,32,512]{2,1,0:T(8,128)(2,1)S(1)} collective-permute-done((bf16[32,32,512]{2,1,0:T(8,128)(2,1)S(1)}, bf16[32,32,512]{2,1,0:T(8,128)(2,1)S(1)}, u32[]{:S(2)}, u32[]{:S(2)}) %collective-permute-start.1) | collective-permute-done | bytes 1048608 | tf_op jit(solution)/shard_map/ppermute | solution.py:181
  112.0 0.4 add_convert_fusion
  112.4 33.6 %all_to_all.11 = bf16[32,32,512]{2,1,0:T(8,128)(2,1)S(1)} all-to-all(bf16[32,32,512]{2,1,0:T(8,128)(2,1)S(1)} %add_convert_fusion), channel_id=1, replica_groups=mesh['row'=4,'col'=16,'zhi'=2,'core'=2] {'col','zhi'}, dimensions={0} | all-to-all | bytes 2097152 | tf_op jit(solution)/shard_map/all_to_all | solution.py:183
  146.0 0.2 convert_reduce_fusion.1
  146.2 0.0 copy-done.4
  146.2 0.0 copy-done.6
  146.2 0.0 copy-done.8
  146.2 6.3 %bitcast_reduce_fusion = (f32[512,32]{0,1:T(8,128)S(1)}, f32[512,32]{0,1:T(8,128)S(1)}, f32[32,512,128]{1,2,0:T(8,128)S(1)}) fusion(f32[128]{0:T(128)S(1)} %copy-done.10, f32[512,32]{0,1:T(8,128)S(1)} %copy-done.8, f32[512,32]{0,1:T(8,128)S(1)} %copy-done.6, bf16[512,32,128]{0,2,1:T(8,128)(2,1)S(1)} %copy-done.4, bf16[128,16]{0,1:T(8,128)(2,1)S(1)} %copy-done.11, ...), kind=kOutput, calls=%fused_computation.14 | convolution fusion | flops 417300480 | bytes 13898240 | tf_op jit(solution)/shard_map/hwr,ch->rwc/dot_general | solution.py:185
  152.6 4.3 %fusion.9 = bf16[512,32,128]{0,2,1:T(8,128)(2,1)} fusion(bf16[512,32,128]{0,2,1:T(8,128)(2,1)S(1)} %copy-done.4, f32[32,512,128]{1,2,0:T(8,128)S(1)} %get-tuple-element.19, f32[512,32]{0,1:T(8,128)S(1)} %get-tuple-element.20, f32[512,32]{0,1:T(8,128)S(1)} %get-tuple-element.21, f32[128]{0:T(128)S(1)} %copy-done.10, f32[512,32]{0,1:T(8,128)S(1)} %copy-done.8, ...), kind=kLoop, calls=%fused_computation.11 | loop fusion | flops 18874368 | bytes 17039872 | tf_op jit(solution)/shard_map/convert_element_type | solution.py:186
  156.9 7.8 %copy.24 = bf16[512,32,128]{2,1,0:T(8,128)(2,1)} copy(bf16[512,32,128]{0,2,1:T(8,128)(2,1)} %fusion.9) | data formatting | bytes 8388608
  (5 shorter events, 0.1 us)
Async XLA Ops:
  7.2 58.9 %copy-start = (bf16[10,1,48,2048]{3,2,1,0:T(8,128)(2,1)S(1)}, bf16[10,1,48,2048]{3,2,1,0:T(8,128)(2,1)}, u32[]{:S(2)}) copy-start(bf16[10,1,48,2048]{3,2,1,0:T(8,128)(2,1)} %param.15) | copy-start | bytes 5898244
  7.2 61.6 %all-gather.3.cloned.1.call-start = ((), (), s32[]{:S(2)}) async-start(), calls=%async_computation.2 | async-start | bytes 5160960 | tf_op jit(solution)/shard_map/all_gather | solution.py:159
  10.4 14.2 %copy-start.10 = (f32[128]{0:T(128)S(1)}, f32[128]{0:T(128)}, u32[]{:S(2)}) copy-start(f32[128]{0:T(128)} %param.10) | copy-start | bytes 1540
  10.4 14.2 %copy-start.11 = (bf16[128,16]{0,1:T(8,128)(2,1)S(1)}, bf16[128,16]{0,1:T(8,128)(2,1)}, u32[]{:S(2)}) copy-start(bf16[128,16]{0,1:T(8,128)(2,1)} %param.11) | copy-start | bytes 12292
  17.9 6.8 %copy-start.3 = (bf16[512,32,128]{0,2,1:T(8,128)(2,1)S(1)}, bf16[512,32,128]{0,2,1:T(8,128)(2,1)}, u32[]{:S(2)}) copy-start(bf16[512,32,128]{0,2,1:T(8,128)(2,1)} %copy.18) | copy-start | bytes 12582916
  21.0 45.0 %copy-start.5 = (f32[512,32]{0,1:T(8,128)}, f32[512,32]{0,1:T(8,128)S(1)}, u32[]{:S(2)}) copy-start(f32[512,32]{0,1:T(8,128)S(1)} %broadcast_multiply_fusion.2) | copy-start | bytes 196612
  21.0 45.0 %copy-start.9 = (s32[2048]{0:T(1024)S(1)}, s32[2048]{0:T(1024)}, u32[]{:S(2)}) copy-start(s32[2048]{0:T(1024)} %param.17) | copy-start | bytes 24580
  24.7 41.3 %copy-start.7 = (f32[512,32]{0,1:T(8,128)}, f32[512,32]{0,1:T(8,128)S(1)}, u32[]{:S(2)}) copy-start(f32[512,32]{0,1:T(8,128)S(1)} %add_rsqrt_fusion) | copy-start | bytes 196612
  26.1 42.7 %copy-start.1 = (bf16[10,1,48,512]{3,2,1,0:T(8,128)(2,1)S(1)}, bf16[10,1,48,512]{3,2,1,0:T(8,128)(2,1)}, u32[]{:S(2)}) copy-start(bf16[10,1,48,512]{3,2,1,0:T(8,128)(2,1)} %param.12) | copy-start | bytes 1474564
  66.0 2.8 %collective-permute-start = (bf16[32,32,512]{2,1,0:T(8,128)(2,1)S(1)}, bf16[32,32,512]{2,1,0:T(8,128)(2,1)}, u32[]{:S(2)}, u32[]{:S(2)}) collective-permute-start(bf16[32,32,512]{2,1,0:T(8,128)(2,1)S(1)} %all_to_all.10.mine_ref), channel_id=1, source_target_pairs={{0,1},{1,0},{2,3},{3,2},{4,5},{5,4},{6,7},{7,6},{8,9},{9,8},{10,11... | collective-permute-start | bytes 3145736 | tf_op jit(solution)/shard_map/ppermute | solution.py:168
  68.8 1.0 copy-start.2
  69.8 76.4 %copy-start.4 = (bf16[512,32,128]{0,2,1:T(8,128)(2,1)S(1)}, bf16[512,32,128]{0,2,1:T(8,128)(2,1)}, u32[]{:S(2)}) copy-start(bf16[512,32,128]{0,2,1:T(8,128)(2,1)} %copy.18) | copy-start | bytes 12582916
  69.8 76.4 %copy-start.6 = (f32[512,32]{0,1:T(8,128)S(1)}, f32[512,32]{0,1:T(8,128)}, u32[]{:S(2)}) copy-start(f32[512,32]{0,1:T(8,128)} %copy-done.5) | copy-start | bytes 196612
  69.8 76.4 %copy-start.8 = (f32[512,32]{0,1:T(8,128)S(1)}, f32[512,32]{0,1:T(8,128)}, u32[]{:S(2)}) copy-start(f32[512,32]{0,1:T(8,128)} %copy-done.7) | copy-start | bytes 196612
  109.4 2.7 %collective-permute-start.1 = (bf16[32,32,512]{2,1,0:T(8,128)(2,1)S(1)}, bf16[32,32,512]{2,1,0:T(8,128)(2,1)S(1)}, u32[]{:S(2)}, u32[]{:S(2)}) collective-permute-start(bf16[32,32,512]{2,1,0:T(8,128)(2,1)S(1)} %get-tuple-element.10), channel_id=1, source_target_pairs={{0,1},{1,0},{2,3},{3,2},{4,5},{5,4},{6,7},{7,6},{8,9},{9,8},{10,11... | collective-permute-start | bytes 3145736 | tf_op jit(solution)/shard_map/ppermute | solution.py:181
Sparse Core Ops, SparseCore 0:
  10.5 53.1 all-gather.2

commit v2 on v1

v2 whole, which is shorter than its diff:
```python
import math

import jax
import jax.numpy as jnp
from jax import lax
from jax.experimental import pallas as pl
from jax.experimental.pallas import tpu as pltpu
from jax.sharding import Mesh, PartitionSpec as P

F32, BF16 = jnp.float32, jnp.bfloat16
EPS = 1e-05
LOG2E = 1.4426950408889634
NEG = -1e9
GROUP = 8


def split(x):
    hi = x.astype(BF16)
    return hi, (x - hi.astype(F32)).astype(BF16)


def spread(w):
    rows, c = w.shape
    tall = jnp.broadcast_to(w[:, None, :], (rows, GROUP, c)).reshape(rows * GROUP, c)
    line = lax.broadcasted_iota(jnp.int32, tall.shape, 0) % GROUP
    return jnp.concatenate([jnp.where(line == j, tall, 0.0) for j in range(GROUP)], 1)


def bias_kernel(pair_ref, gain_ref, weight_ref, out_ref, hat_ref, inv_ref, x_s):
    rows, width, chan = pair_ref.shape
    heads, copies = out_ref.shape[:2]
    pitch = width + 1
    for i in range(rows):
        x_s[i * pitch:i * pitch + width, :] = pair_ref[i].astype(F32)
    gain = jnp.broadcast_to(gain_ref[...], (GROUP, chan)).T[:, 0:1]
    weight = spread(weight_ref[...].astype(F32)).astype(BF16)
    found = []
    for g in range(width // GROUP):
        cols = []
        for j in range(g * GROUP, (g + 1) * GROUP):
            x = x_s[pl.ds(j, rows, stride=pitch), :].astype(BF16).T.astype(F32)
            cen = x - jnp.mean(x, axis=0, keepdims=True)
            inv = lax.rsqrt(jnp.mean(cen * cen, axis=0, keepdims=True) + EPS)
            hat = cen * inv
            inv_ref[j:j + 1, :] = inv
            hat_ref[j] = hat.astype(BF16)
            cols.append((hat * gain).astype(BF16))
        tile = jnp.dot(weight, jnp.concatenate(cols, 0), preferred_element_type=F32)
        found.append(tile.reshape(heads, GROUP, rows))
    for g in range(0, width // GROUP, 2):
        both = jnp.concatenate(found[g:g + 2], 1).astype(BF16)
        for z in range(copies):
            out_ref[:, z, g * GROUP:(g + 2) * GROUP, :] = both


def pair_bias(pair, gain, weight, copies, block=256):
    I, W, C = pair.shape
    H = weight.shape[1]
    return pl.pallas_call(
        bias_kernel,
        grid=(I // block,),
        in_specs=[pl.BlockSpec((block, W, C), lambda n: (n, 0, 0)),
                  pl.BlockSpec((1, C), lambda n: (0, 0)),
                  pl.BlockSpec((H, C), lambda n: (0, 0))],
        out_specs=[pl.BlockSpec((H, copies, W, block), lambda n: (0, 0, 0, n)),
                   pl.BlockSpec((W, C, block), lambda n: (0, 0, n)),
                   pl.BlockSpec((W, block), lambda n: (0, n))],
        out_shape=[jax.ShapeDtypeStruct((H, copies, W, I), BF16),
                   jax.ShapeDtypeStruct((W, C, I), BF16),
                   jax.ShapeDtypeStruct((W, I), F32)],
        scratch_shapes=[pltpu.VMEM((block * (W + 1), C), F32)],
        compiler_params=pltpu.CompilerParams(vmem_limit_bytes=32 * 1024 * 1024),
        cost_estimate=pl.CostEstimate(flops=20 << 30, bytes_accessed=40 << 20, transcendentals=0),
        name="pair_bias",
    )(pair, gain.reshape(1, C), weight.T)


def grad_kernel(part_ref, bias_ref, inv_ref, hat_ref, weight_ref, out_ref, y_s):
    rows, width, chan = out_ref.shape
    heads = bias_ref.shape[0]
    copies = part_ref.shape[0] // heads
    pitch = width + 1
    grads = part_ref[...].astype(F32).reshape(heads, copies, width, rows).sum(axis=1)
    inv = inv_ref[...]
    tilt = jnp.sum(grads * bias_ref[:, 0].astype(F32), axis=0) * (inv * (1.0 / chan))
    grads = grads * inv[None]
    for g in range(width // GROUP):
        part = grads[:, g * GROUP:(g + 1) * GROUP, :].reshape(heads * GROUP, rows)
        hi, lo = split(part)
        scaled = jnp.dot(weight_ref[...], jnp.concatenate([hi, lo, hi], 0), preferred_element_type=F32)
        for n in range(GROUP):
            j = g * GROUP + n
            d = scaled[n * chan:(n + 1) * chan] - tilt[j:j + 1, :] * hat_ref[j].astype(F32)
            y_s[pl.ds(j, rows, stride=pitch), :] = d.astype(BF16).T.astype(F32)
    for i in range(rows):
        out_ref[i] = y_s[i * pitch:i * pitch + width, :].astype(BF16)


def pair_grad(parts, bias, inv, hat, weight, block=256):
    W, C, I = hat.shape
    H, copies = bias.shape[:2]
    whole = lambda a: pl.BlockSpec(a.shape, lambda n: (0,) * a.ndim)
    return pl.pallas_call(
        grad_kernel,
        grid=(I // block,),
        in_specs=[pl.BlockSpec((H * copies, W, block), lambda n: (0, 0, n)),
                  pl.BlockSpec((H, 1, W, block), lambda n: (0, 0, 0, n)),
                  pl.BlockSpec((W, block), lambda n: (0, n)),
                  pl.BlockSpec((W, C, block), lambda n: (0, 0, n)),
                  whole(weight)],
        out_specs=pl.BlockSpec((block, W, C), lambda n: (n, 0, 0)),
        out_shape=jax.ShapeDtypeStruct((I, W, C), BF16),
        scratch_shapes=[pltpu.VMEM((block * (W + 1), C), F32)],
        compiler_params=pltpu.CompilerParams(vmem_limit_bytes=32 * 1024 * 1024),
        cost_estimate=pl.CostEstimate(flops=10 << 30, bytes_accessed=20 << 20, transcendentals=0),
        name="pair_grad",
    )(parts, bias, inv, hat, weight)


def grad_weight(weight, gain):
    scaled = weight.astype(F32) * gain[:, None]
    hi, lo = split((scaled - jnp.mean(scaled, axis=0, keepdims=True)).T)
    return jnp.concatenate([spread(w.astype(F32)).astype(BF16) for w in (hi, hi, lo)], 0).T


def attend_kernel(core_ref, mine_ref, other_ref, mask_ref, q_ref, k_ref, v_ref, g_ref,
                  o_ref, dq_ref, keep_ref, send_ref,
                  bias_s, acc_s, s0_s, s1_s, e0_s, e1_s, kt_s, vt_s, kc_s, g2_s, mask_s):
    step = pl.program_id(0)
    steps = pl.num_programs(0)
    n_i = q_ref.shape[-1]
    dh = q_ref.shape[-2]
    n_j = bias_s.shape[0]
    rows = k_ref.shape[0]
    per = JT = n_j // rows
    core = core_ref[0]
    blocks = mine_ref.shape[0]
    bj = mine_ref.shape[1]
    scaling = 1.0 / math.sqrt(dh)
    IH = n_i // 2
    half = (slice(0, IH), slice(IH, 2 * IH))
    s_s = (s0_s, s1_s)
    e_s = (e0_s, e1_s)

    def position(b, parity):
        return pl.ds(pl.multiple_of((b * 2 + parity) * bj, bj), bj)

    @pl.when(step == 0)
    def _():
        mask_s[...] = jnp.concatenate([mask_ref[r, 0, :16, :].astype(F32) for r in range(rows)], 1).T

        @pl.loop(0, blocks, unroll=4)
        def _(b):
            for src, par in ((mine_ref, core), (other_ref, 1 - core)):
                at = position(b, par)
                bias_s[at, :] = jnp.where(mask_s[at, 0:1] > 0, src[b].astype(F32) * LOG2E, NEG)
                acc_s[at, :] = jnp.zeros((bj, n_i), F32)

        e1_s[...] = jnp.zeros_like(e1_s)
        vt_s[...] = jnp.zeros_like(vt_s)
        g2_s[...] = jnp.zeros_like(g2_s)
        kc_s[...] = jnp.zeros_like(kc_s)

    tiles = range(0, n_j, JT)

    def scores(h):
        il = half[h]
        q = q_ref[0, :, il].astype(F32) * (scaling * LOG2E)
        qh = q.astype(BF16)
        ql = (q - qh.astype(F32)).astype(BF16)
        q2 = jnp.concatenate([qh, ql], 0)
        m = None
        for t in tiles:
            s = jnp.dot(kt_s[t:t + JT, :], q2, preferred_element_type=F32) + bias_s[t:t + JT, il]
            s_s[h][t:t + JT, :] = s
            mt = jnp.max(s.reshape(JT // 8, 8, IH), axis=0)
            m = mt if m is None else jnp.maximum(m, mt)
            yield None
        yield jnp.max(m, axis=0, keepdims=True)

    def soften(h, m):
        il = half[h]
        o = None
        one = jnp.ones((16, JT), BF16)
        for t in tiles:
            e = jnp.exp2(s_s[h][t:t + JT, :] - m).astype(BF16)
            e_s[h][t:t + JT, :] = e
            v = v_ref[t // per, 0]
            ot = jnp.dot(jnp.concatenate([v, one], 0), e, preferred_element_type=F32)
            o = ot if o is None else o + ot
            yield None
        inv = 1.0 / o[dh:dh + 1, :]
        o = o[:dh] * inv
        o_ref[0, :, il] = o.astype(BF16)
        g = g_ref[0, :, il].astype(F32)
        centre = jnp.sum(g * o, axis=0, keepdims=True)
        g = g * inv
        c = -centre * inv
        gh = g.astype(BF16)
        gl = (g - gh.astype(F32)).astype(BF16)
        ch = c.astype(BF16).astype(F32)
        cl = c - ch
        line = lax.broadcasted_iota(jnp.int32, (16, IH), 0)
        cb = jnp.where(line == 0, ch, jnp.where(line == 1, cl, 0.0)).astype(BF16)
        yield jnp.concatenate([gh, gl, cb], 0)

    def backward(h, at, g2):
        il = half[h]
        dq = None
        for t in tiles:
            x = jnp.dot(vt_s[t:t + JT, :], g2, preferred_element_type=F32)
            ds = e_s[h][t:t + JT, :].astype(F32) * x
            acc_s[t:t + JT, il] += ds
            dt = jnp.dot(kc_s[:, t:t + JT], ds.astype(BF16), preferred_element_type=F32)
            dq = dt if dq is None else dq + dt
            yield None
        dq_ref[at, :, il] = (dq * scaling).astype(BF16)
        yield None

    def together(*chains):
        last = [None] * len(chains)
        live = list(range(len(chains)))
        while live:
            for n in list(live):
                try:
                    last[n] = next(chains[n])
                except StopIteration:
                    live.remove(n)
        return last

    for r in range(rows):
        sl = slice(r * per, (r + 1) * per)
        kz = k_ref[r, 0] * mask_ref[r, 0]
        kt_s[sl, :] = jnp.concatenate([kz, kz], 0).T
    m0, _ = together(scores(0), backward(1, jnp.maximum(step - 1, 0), g2_s[...]))
    for r in range(rows):
        sl = slice(r * per, (r + 1) * per)
        v = v_ref[r, 0]
        vt_s[sl, :] = jnp.concatenate([v, v, jnp.ones((16, per), BF16)], 0).T
        kc_s[:, sl] = k_ref[r, 0]
    g20, m1 = together(soften(0, m0), scores(1))
    _, g21 = together(backward(0, step, g20), soften(1, m1))
    g2_s[...] = g21

    @pl.when(step == steps - 1)
    def _():
        together(backward(1, step, g2_s[...]))

        @pl.loop(0, blocks, unroll=4)
        def _(b):
            for dst, par in ((keep_ref, core), (send_ref, 1 - core)):
                dst[b] = acc_s[position(b, par), :].astype(BF16)


def attention(core, mine, other, q, kv, g):
    S, dh, I = q.shape
    R, per = kv.shape[0], kv.shape[3]
    J = R * per
    IH = I // 2
    full = lambda a: pl.BlockSpec(a.shape, lambda s: (0,) * a.ndim)
    one = pl.BlockSpec((1, dh, I), lambda s: (s, 0, 0))
    all_rows = lambda at: pl.BlockSpec((R, 1, dh, per), lambda s: (0, at(s), 0, 0))
    return pl.pallas_call(
        attend_kernel,
        grid=(S,),
        in_specs=[pl.BlockSpec(memory_space=pltpu.SMEM), full(mine), full(other), all_rows(lambda s: 2 * S),
                  one, all_rows(lambda s: s), all_rows(lambda s: s + S), one],
        out_specs=[one, full(q), full(mine), full(other)],
        out_shape=[jax.ShapeDtypeStruct(a.shape, BF16) for a in (q, q, mine, other)],
        scratch_shapes=[pltpu.VMEM((J, I), F32), pltpu.VMEM((J, I), F32),
                        pltpu.VMEM((J, IH), F32), pltpu.VMEM((J, IH), F32),
                        pltpu.VMEM((J, IH), BF16), pltpu.VMEM((J, IH), BF16),
                        pltpu.VMEM((J, 2 * dh), BF16), pltpu.VMEM((J, 2 * dh + 16), BF16),
                        pltpu.VMEM((dh, J), BF16), pltpu.VMEM((2 * dh + 16, IH), BF16),
                        pltpu.VMEM((J, 16), F32)],
        compiler_params=pltpu.CompilerParams(vmem_limit_bytes=32 * 1024 * 1024),
        cost_estimate=pl.CostEstimate(flops=8 * S * J * I * dh, bytes_accessed=12 << 20, transcendentals=S * I * J),
        name="attend",
    )(core, mine, other, kv, q, kv, kv, g)


def pack_kernel(k_ref, v_ref, m_ref, out_ref):
    S = k_ref.shape[0]
    out_ref[:S] = k_ref[...]
    out_ref[S:2 * S] = v_ref[...]
    out_ref[2 * S] = jnp.broadcast_to(m_ref[...].astype(F32), out_ref.shape[1:]).astype(BF16)


def pack(k, v, mask):
    S, dh, per = k.shape
    return pl.pallas_call(
        pack_kernel,
        out_shape=jax.ShapeDtypeStruct((2 * S + 1, dh, per), BF16),
        compiler_params=pltpu.CompilerParams(vmem_limit_bytes=8 * 1024 * 1024),
        name="pack",
    )(k, v, mask.reshape(1, per))


def local(pair, pair_gain, pair_weight, queries, keys, values, d_atoms, key_mask, atom_token):
    strip = queries.shape[3]
    swap = lambda x: lax.ppermute(x, "core", [(0, 1), (1, 0)])
    spread_out = lambda x: lax.all_to_all(x, ("col", "zhi"), 0, 0, tiled=True)

    kv = lax.all_gather(pack(keys[:, 0], values[:, 0], key_mask), "row")
    bias, hat, inv = pair_bias(pair, pair_gain, pair_weight, lax.axis_size("zhi"))
    heads, copies, width, _ = bias.shape
    mine = spread_out(bias.reshape(heads * copies, width, strip))
    other = swap(mine)

    offset = lax.axis_index("row") * strip
    onehot = (
        atom_token[:, None] - offset == jnp.arange(strip, dtype=jnp.int32)[None, :]
    ).astype(BF16)
    grad_out = jnp.einsum(
        "sda,at->sdt", d_atoms[:, 0], onehot, preferred_element_type=F32
    ).astype(BF16)

    core = lax.axis_index("core").astype(jnp.int32).reshape(1)
    weight = grad_weight(pair_weight, pair_gain)
    kv, weight = lax.optimization_barrier((kv, weight))
    o, dq, keep, send = attention(core, mine, other, queries[:, 0], kv, grad_out)

    chip = (keep.astype(F32) + swap(send).astype(F32)).astype(BF16)
    d_pair = pair_grad(spread_out(chip), bias, inv, hat, weight)
    return (o[:, None], dq[:, None], d_pair)


def solution(mesh):
    fine = Mesh(mesh.devices.reshape(4, 16, 2, 2), ("row", "col", "zhi", "core"))
    sample = ("zhi", "core")
    tokens = P(sample, "col", None, "row")
    tile = P("row", ("col", "zhi", "core"), None)
    return jax.shard_map(
        local,
        mesh=fine,
        in_specs=(tile, P(), P(), tokens, tokens, tokens, tokens, P("row"), P("row")),
        out_specs=(tokens, tokens, tile),
        check_vma=False,
    )
```

time: 172 us -> 154 us (0.90)
  blocking collectives: 73.1 us -> 36.2 us
  waiting for transfers between devices: 3.15 us -> 25.8 us
  starting transfers between devices: 0.15 us -> 12.4 us
  matrix products: 9.86 us -> 2.16 us
  other arithmetic: 14.7 us -> 7.74 us
  local copies, waits for them, and re-layouts: 16.8 us -> 11.2 us
  Pallas kernels: 39.5 us -> 44 us
    all_to_all x2 -> x1, blocking collectives: 73.1 us -> 36.2 us  [local(): spread_out = lambda x: lax.all_to_all(x, ('col', 'zhi'), 0, 0, tiled=True)]
    all_to_all x0 -> x1, waiting for transfers between devices: none -> 23.5 us  [local(): spread_out = lambda x: lax.all_to_all(x, ('col', 'zhi'), 0, 0, tiled=True)]
    all_to_all x0 -> x1, starting transfers between devices: none -> 11.8 us  [local(): spread_out = lambda x: lax.all_to_all(x, ('col', 'zhi'), 0, 0, tiled=True)]
    dot_general x2 -> x0, matrix products: 7.7 us -> none  [the longest x1 6.32 us: local(): jnp.einsum('hwr,ch->rwc', tile_grad, pair_weight.astype(F32), precision=H...]
    reduce_sum x3 -> x1, other arithmetic: 6.85 us -> 0.11 us  [grad_weight(): hi, lo = split((scaled - jnp.mean(scaled, axis=0, keepdims=True)).T)]
    unnamed x26 -> x32, local copies, waits for them, and re-layouts: 16.4 us -> 10.9 us
    convert_element_type x3, other arithmetic: 5.48 us -> 0.53 us  [the longest x1 0.38 us: local(): chip = (keep.astype(F32) + swap(send).astype(F32)).astype(BF16)]
    pallas_call x1 -> x4, Pallas kernels: 39.5 us -> 44 us  [the longest x1 32.2 us: attention(): pl.pallas_call(attend_kernel, grid=(S,), in_specs=[pl.BlockSpec(memory_sp...]
  transfers between devices with their start and end apart: 3 -> 4, of which waited for: 2 -> 2; matrix products, arithmetic and copies ran while one was open for 11% -> 6% of each run, Pallas kernels for 0% -> 3%
where the time goes in v2:
time: 154 us
  Pallas kernels  44 us (29%)
  blocking collectives  36.2 us (24%)
  waiting for transfers between devices  25.8 us (17%)
  between operations  14.2 us (9%)
  starting transfers between devices  12.4 us (8%)
  local copies, waits for them, and re-layouts  11.2 us (7%)
  other arithmetic  7.74 us (5%)
  matrix products  2.16 us (1%)
    all_to_all x1, blocking collectives, local(): spread_out = lambda x: lax.all_to_all(x, ('col', 'zhi'), 0, 0, tiled=True)  36.2 us
    pallas_call x1, Pallas kernels, attention(): pl.pallas_call(attend_kernel, grid=(S,), in_specs=[pl.BlockSpec(memory_sp...  32.2 us
    all_to_all x1, waiting for transfers between devices, local(): spread_out = lambda x: lax.all_to_all(x, ('col', 'zhi'), 0, 0, tiled=True)  23.5 us
    all_to_all x1, starting transfers between devices, local(): spread_out = lambda x: lax.all_to_all(x, ('col', 'zhi'), 0, 0, tiled=True)  11.8 us
    unnamed x32, local copies, waits for them, and re-layouts  10.9 us
    pallas_call x1, Pallas kernels, pair_grad(): pl.pallas_call(grad_kernel, grid=(I // block,), in_specs=[pl.BlockSpec((H...  5.55 us
    pallas_call x1, Pallas kernels, pair_bias(): pl.pallas_call(bias_kernel, grid=(I // block,), in_specs=[pl.BlockSpec((b...  5.23 us
    unnamed x13, other arithmetic  3.87 us
  transfers between devices with their start and end apart: 4, of which 2 were waited for; matrix products, arithmetic and copies ran while one was open for 6% of the time, Pallas kernels for 3%

profile of v2, /device:TPU:8, one launch (start us, length us, event | category | flops | bytes accessed | tf_op | source)
XLA Modules:
  0.0 153.7 jit_solution(1720033512445173336)
XLA Ops:
  7.2 0.0 copy-start
  7.2 0.0 copy-start.5
  7.2 0.0 copy-start.4
  7.2 0.0 all-gather.3.cloned.1.call-start
  7.2 0.0 copy-start.2
  7.3 1.1 copy-done.2
  8.4 0.0 copy-start.3
  8.4 1.0 copy-done.3
  9.4 0.0 copy-start.6
  9.4 0.7 copy-done.6
  10.1 1.0 pack.1
  11.2 0.0 all-gather.3.cloned.1.call-update
  11.2 0.0 copy-done.5
  11.2 0.0 copy-done.4
  11.2 0.0 copy-start.7
  11.2 2.2 %copy-done.7 = bf16[512,32,128]{2,1,0:T(8,128)(2,1)S(1)} copy-done((bf16[512,32,128]{2,1,0:T(8,128)(2,1)S(1)}, bf16[512,32,128]{2,1,0:T(8,128)(2,1)}, u32[]{:S(2)}) %copy-start.7) | copy-done | bytes 4194328
  13.4 5.2 %pair_bias.1 = (bf16[16,2,32,512]{3,2,1,0:T(8,128)(2,1)}, bf16[32,128,512]{2,1,0:T(8,128)(2,1)S(1)}, f32[32,512]{1,0:T(8,128)S(1)}) custom-call(bf16[512,32,128]{2,1,0:T(8,128)(2,1)S(1)} %copy-done.7, f32[1,128]{1,0:T(1,128)S(1)} %bitcast.51, bf16[16,128]{1,0:T(8,128)(2,1)S(1)} %bitcast.50), custom_call_target="tpu_custom_call" | custom-call | flops 21474836480 | bytes 41943040 | tf_op jit(solution)/shard_map/pair_bias/pallas_call | solution.py:59
  18.6 0.0 copy-start.11
  18.6 2.0 %copy-done.11 = bf16[32,128,512]{2,1,0:T(8,128)(2,1)} copy-done((bf16[32,128,512]{2,1,0:T(8,128)(2,1)}, bf16[32,128,512]{2,1,0:T(8,128)(2,1)S(1)}, u32[]{:S(2)}) %copy-start.11) | copy-done | bytes 4194328
  20.6 0.0 copy-start.13
  20.6 0.6 copy-done.13
  21.3 0.0 copy-start.15
  21.3 11.8 %all-to-all-start = ((bf16[32,32,512]{2,1,0:T(8,128)(2,1)}), bf16[32,32,512]{2,1,0:T(8,128)(2,1)S(1)}, u32[]{:S(2)}, u32[]{:S(2)}) async-start(bf16[32,32,512]{2,1,0:T(8,128)(2,1)} %bitcast.3), calls=%async_computation | async-start | bytes 2097152 | tf_op jit(solution)/shard_map/all_to_all | solution.py:302
  33.1 0.1 fusion.49
  33.2 0.1 fusion.51
  33.3 0.1 copy.34
  33.4 0.1 fusion.50
  33.5 0.1 copy.42
  33.8 0.6 constant_dynamic-update-slice_fusion
  34.5 0.6 constant_dynamic-update-slice_fusion.14
  35.1 0.6 constant_dynamic-update-slice_fusion.13
  35.7 0.6 constant_dynamic-update-slice_fusion.12
  36.3 0.6 constant_dynamic-update-slice_fusion.11
  37.0 0.6 constant_dynamic-update-slice_fusion.10
  37.6 23.5 %all-to-all-done.mine_ref = bf16[32,32,512]{2,1,0:T(8,128)(2,1)S(1)} async-done(((bf16[32,32,512]{2,1,0:T(8,128)(2,1)}), bf16[32,32,512]{2,1,0:T(8,128)(2,1)S(1)}, u32[]{:S(2)}, u32[]{:S(2)}) %all-to-all-start) | async-done | bytes 1048608 | tf_op jit(solution)/shard_map/all_to_all | solution.py:302
  61.1 0.0 collective-permute-start
  61.1 0.6 constant_dynamic-update-slice_fusion.9
  61.7 0.6 constant_dynamic-update-slice_fusion.8
  62.3 2.0 %maximum_bitcast_fusion.weight_ref = bf16[1024,384]{1,0:T(8,128)(2,1)} fusion(bf16[128,1024]{0,1:T(8,128)(2,1)} %constant_dynamic-update-slice_fusion.8, bf16[128,1024]{0,1:T(8,128)(2,1)S(1)} %get-tuple-element.30), kind=kLoop, calls=%fused_computation.8 | loop fusion | flops 2359296 | bytes 1310720 | tf_op jit(solution)/shard_map/transpose | solution.py:123
  64.3 0.0 copy-done.15
  64.3 0.0 copy-done
  64.3 0.0 copy-start.9
  64.3 2.2 %fusion.10.g_ref = bf16[10,48,512]{2,1,0:T(8,128)(2,1)} fusion(bf16[10,1,48,2048]{3,2,1,0:T(8,128)(2,1)S(1)} %copy-done, s32[2048]{0:T(1024)S(1)} %broadcast_subtract_fusion), kind=kOutput, calls=%fused_computation.7 | convolution fusion | flops 1007927296 | bytes 2465792 | tf_op jit(solution)/shard_map/sda,at->sdt/dot_general | solution.py:314
  66.4 0.0 all-gather.3.cloned.1.call-done
  66.5 0.0 collective-permute-done.other_ref
  66.5 0.0 copy-done.9
  66.5 0.0 copy-start.8
  66.5 2.2 %copy-done.8 = bf16[84,48,512]{2,1,0:T(8,128)(2,1)S(1)} copy-done((bf16[84,48,512]{2,1,0:T(8,128)(2,1)S(1)}, bf16[84,48,512]{2,1,0:T(8,128)(2,1)}, u32[]{:S(2)}) %copy-start.8) | copy-done | bytes 4128792
  68.6 0.0 copy-start.10
  68.6 1.0 copy-done.10
  69.7 32.2 %attend.1 = (bf16[10,48,512]{2,1,0:T(8,128)(2,1)}, bf16[10,48,512]{2,1,0:T(8,128)(2,1)}, bf16[32,32,512]{2,1,0:T(8,128)(2,1)S(1)}, bf16[32,32,512]{2,1,0:T(8,128)(2,1)S(1)}) custom-call(s32[1]{0:T(128)} %bitcast.core_ref, bf16[32,32,512]{2,1,0:T(8,128)(2,1)S(1)} %all-to-all-done.mine_ref, bf16[32,32,512]{2,1,0:T(8,128)(2,1)} %collective-permute-done.other_ref, ...), custom_call_target="tpu_custom_call" | custom-call | flops 4026531840 | bytes 12582912 | tf_op jit(solution)/shard_map/attend/pallas_call | solution.py:263
  101.9 0.5 collective-permute-start.1
  102.4 2.3 %collective-permute-done.1 = bf16[32,32,512]{2,1,0:T(8,128)(2,1)S(1)} collective-permute-done((bf16[32,32,512]{2,1,0:T(8,128)(2,1)S(1)}, bf16[32,32,512]{2,1,0:T(8,128)(2,1)S(1)}, u32[]{:S(2)}, u32[]{:S(2)}) %collective-permute-start.1) | collective-permute-done | bytes 1048608 | tf_op jit(solution)/shard_map/ppermute | solution.py:301
  104.6 0.0 copy-start.1
  104.6 0.0 copy-start.12
  104.7 0.0 copy-start.14
  104.7 0.4 add_convert_fusion
  105.0 36.2 %all_to_all.10.part_ref = bf16[32,32,512]{2,1,0:T(8,128)(2,1)S(1)} all-to-all(bf16[32,32,512]{2,1,0:T(8,128)(2,1)S(1)} %add_convert_fusion), channel_id=1, replica_groups=mesh['row'=4,'col'=16,'zhi'=2,'core'=2] {'col','zhi'}, dimensions={0} | all-to-all | bytes 2097152 | tf_op jit(solution)/shard_map/all_to_all | solution.py:302
  141.3 0.0 copy-done.1
  141.3 0.0 copy-done.12
  141.3 0.0 copy-done.14
  141.3 5.6 %pair_grad.1 = bf16[512,32,128]{2,1,0:T(8,128)(2,1)} custom-call(bf16[32,32,512]{2,1,0:T(8,128)(2,1)S(1)} %all_to_all.10.part_ref, bf16[16,2,32,512]{3,2,1,0:T(8,128)(2,1)} %get-tuple-element.12.bias_ref, f32[32,512]{1,0:T(8,128)S(1)} %copy-done.14, bf16[32,128,512]{2,1,0:T(8,128)(2,1)S(1)} %copy-done.12, bf16[1024,384]{1,0:T(8,128)(2,1)S(1)} %copy-done.1), custom_call_target="tpu_custom_call" | custom-call | flops 10737418240 | bytes 20971520 | tf_op jit(solution)/shard_map/pair_grad/pallas_call | solution.py:103
  (13 shorter events, 0.2 us)
Async XLA Ops:
  7.2 57.1 %copy-start = (bf16[10,1,48,2048]{3,2,1,0:T(8,128)(2,1)S(1)}, bf16[10,1,48,2048]{3,2,1,0:T(8,128)(2,1)}, u32[]{:S(2)}) copy-start(bf16[10,1,48,2048]{3,2,1,0:T(8,128)(2,1)} %param.15) | copy-start | bytes 5898244
  7.2 4.0 %copy-start.5 = (f32[128]{0:T(128)S(1)}, f32[128]{0:T(128)}, u32[]{:S(2)}) copy-start(f32[128]{0:T(128)} %param.10) | copy-start | bytes 1540
  7.2 4.0 %copy-start.4 = (bf16[128,16]{0,1:T(8,128)(2,1)S(1)}, bf16[128,16]{0,1:T(8,128)(2,1)}, u32[]{:S(2)}) copy-start(bf16[128,16]{0,1:T(8,128)(2,1)} %param.11) | copy-start | bytes 12292
  7.2 59.2 %all-gather.3.cloned.1.call-start = ((), (), s32[]{:S(2)}) async-start(), calls=%async_computation.2 | async-start | bytes 5160960 | tf_op jit(solution)/shard_map/all_gather | solution.py:304
  7.2 1.2 copy-start.2
  8.4 1.0 copy-start.3
  9.4 0.7 copy-start.6
  11.2 2.2 %copy-start.7 = (bf16[512,32,128]{2,1,0:T(8,128)(2,1)S(1)}, bf16[512,32,128]{2,1,0:T(8,128)(2,1)}, u32[]{:S(2)}) copy-start(bf16[512,32,128]{2,1,0:T(8,128)(2,1)} %pair_ref.1) | copy-start | bytes 12582916
  18.6 2.0 %copy-start.11 = (bf16[32,128,512]{2,1,0:T(8,128)(2,1)}, bf16[32,128,512]{2,1,0:T(8,128)(2,1)S(1)}, u32[]{:S(2)}) copy-start(bf16[32,128,512]{2,1,0:T(8,128)(2,1)S(1)} %get-tuple-element.19.hat_ref) | copy-start | bytes 12582916
  20.6 0.6 copy-start.13
  21.3 43.0 %copy-start.15 = (s32[2048]{0:T(1024)S(1)}, s32[2048]{0:T(1024)}, u32[]{:S(2)}) copy-start(s32[2048]{0:T(1024)} %param.17) | copy-start | bytes 24580
  21.3 39.8 %all-to-all-start = ((bf16[32,32,512]{2,1,0:T(8,128)(2,1)}), bf16[32,32,512]{2,1,0:T(8,128)(2,1)S(1)}, u32[]{:S(2)}, u32[]{:S(2)}) async-start(bf16[32,32,512]{2,1,0:T(8,128)(2,1)} %bitcast.3), calls=%async_computation | async-start | bytes 2097152 | tf_op jit(solution)/shard_map/all_to_all | solution.py:302
  61.1 5.4 %collective-permute-start = (bf16[32,32,512]{2,1,0:T(8,128)(2,1)S(1)}, bf16[32,32,512]{2,1,0:T(8,128)(2,1)}, u32[]{:S(2)}, u32[]{:S(2)}) collective-permute-start(bf16[32,32,512]{2,1,0:T(8,128)(2,1)S(1)} %all-to-all-done.mine_ref), channel_id=1, source_target_pairs={{0,1},{1,0},{2,3},{3,2},{4,5},{5,4},{6,7},{7,6},{8,9},{9,8},{10,11... | collective-permute-start | bytes 3145736 | tf_op jit(solution)/shard_map/ppermute | solution.py:301
  64.3 2.2 %copy-start.9 = (bf16[10,1,48,512]{3,2,1,0:T(8,128)(2,1)S(1)}, bf16[10,1,48,512]{3,2,1,0:T(8,128)(2,1)}, u32[]{:S(2)}) copy-start(bf16[10,1,48,512]{3,2,1,0:T(8,128)(2,1)} %param.12) | copy-start | bytes 1474564
  66.5 2.2 %copy-start.8 = (bf16[84,48,512]{2,1,0:T(8,128)(2,1)S(1)}, bf16[84,48,512]{2,1,0:T(8,128)(2,1)}, u32[]{:S(2)}) copy-start(bf16[84,48,512]{2,1,0:T(8,128)(2,1)} %all-gather.3.cloned.1.call-done) | copy-start | bytes 12386308
  68.6 1.0 copy-start.10
  101.9 2.8 %collective-permute-start.1 = (bf16[32,32,512]{2,1,0:T(8,128)(2,1)S(1)}, bf16[32,32,512]{2,1,0:T(8,128)(2,1)S(1)}, u32[]{:S(2)}, u32[]{:S(2)}) collective-permute-start(bf16[32,32,512]{2,1,0:T(8,128)(2,1)S(1)} %get-tuple-element.17), channel_id=1, source_target_pairs={{0,1},{1,0},{2,3},{3,2},{4,5},{5,4},{6,7},{7,6},{8,9},{9,8},{10,11... | collective-permute-start | bytes 3145736 | tf_op jit(solution)/shard_map/ppermute | solution.py:301
  104.6 36.6 %copy-start.1 = (bf16[1024,384]{1,0:T(8,128)(2,1)S(1)}, bf16[1024,384]{1,0:T(8,128)(2,1)}, u32[]{:S(2)}) copy-start(bf16[1024,384]{1,0:T(8,128)(2,1)} %maximum_bitcast_fusion.weight_ref) | copy-start | bytes 2359300
  104.6 36.6 %copy-start.12 = (bf16[32,128,512]{2,1,0:T(8,128)(2,1)S(1)}, bf16[32,128,512]{2,1,0:T(8,128)(2,1)}, u32[]{:S(2)}) copy-start(bf16[32,128,512]{2,1,0:T(8,128)(2,1)} %copy-done.11) | copy-start | bytes 12582916
  104.7 36.6 %copy-start.14 = (f32[32,512]{1,0:T(8,128)S(1)}, f32[32,512]{1,0:T(8,128)}, u32[]{:S(2)}) copy-start(f32[32,512]{1,0:T(8,128)} %copy-done.13) | copy-start | bytes 196612
Sparse Core Ops, SparseCore 0:
  11.3 53.1 all-gather.2

commit v3 on v2

--- a/solution.py
+++ b/solution.py
@@ -12,6 +12,8 @@
 LOG2E = 1.4426950408889634
 NEG = -1e9
 GROUP = 8
+MASK = 16
+VMEM = 60 * 1024 * 1024
 
 
 def split(x):
@@ -26,31 +28,35 @@
     return jnp.concatenate([jnp.where(line == j, tall, 0.0) for j in range(GROUP)], 1)
 
 
-def bias_kernel(pair_ref, gain_ref, weight_ref, out_ref, hat_ref, inv_ref, x_s):
+def turned(pair_ref, x_s):
     rows, width, chan = pair_ref.shape
-    heads, copies = out_ref.shape[:2]
     pitch = width + 1
     for i in range(rows):
         x_s[i * pitch:i * pitch + width, :] = pair_ref[i].astype(F32)
+    for j in range(width):
+        x = x_s[pl.ds(j, rows, stride=pitch), :].astype(BF16).T.astype(F32)
+        cen = x - jnp.mean(x, axis=0, keepdims=True)
+        inv = lax.rsqrt(jnp.mean(cen * cen, axis=0, keepdims=True) + EPS)
+        yield j, cen * inv, inv
+
+
+def bias_kernel(pair_ref, gain_ref, weight_ref, out_ref, x_s):
+    rows, width, chan = pair_ref.shape
+    heads, copies = out_ref.shape[:2]
     gain = jnp.broadcast_to(gain_ref[...], (GROUP, chan)).T[:, 0:1]
     weight = spread(weight_ref[...].astype(F32)).astype(BF16)
-    found = []
-    for g in range(width // GROUP):
-        cols = []
-        for j in range(g * GROUP, (g + 1) * GROUP):
-            x = x_s[pl.ds(j, rows, stride=pitch), :].astype(BF16).T.astype(F32)
-            cen = x - jnp.mean(x, axis=0, keepdims=True)
-            inv = lax.rsqrt(jnp.mean(cen * cen, axis=0, keepdims=True) + EPS)
-            hat = cen * inv
-            inv_ref[j:j + 1, :] = inv
-            hat_ref[j] = hat.astype(BF16)
-            cols.append((hat * gain).astype(BF16))
-        tile = jnp.dot(weight, jnp.concatenate(cols, 0), preferred_element_type=F32)
-        found.append(tile.reshape(heads, GROUP, rows))
-    for g in range(0, width // GROUP, 2):
-        both = jnp.concatenate(found[g:g + 2], 1).astype(BF16)
-        for z in range(copies):
-            out_ref[:, z, g * GROUP:(g + 2) * GROUP, :] = both
+    cols, found = [], []
+    for j, hat, _ in turned(pair_ref, x_s):
+        cols.append((hat * gain).astype(BF16))
+        if len(cols) == GROUP:
+            tile = jnp.dot(weight, jnp.concatenate(cols, 0), preferred_element_type=F32)
+            found.append(tile.reshape(heads, GROUP, rows))
+            cols = []
+        if len(found) == 2:
+            both = jnp.concatenate(found, 1).astype(BF16)
+            for z in range(copies):
+                out_ref[:, z, j + 1 - 2 * GROUP:j + 1, :] = both
+            found = []
 
 
 def pair_bias(pair, gain, weight, copies, block=256):
@@ -62,17 +68,35 @@
         in_specs=[pl.BlockSpec((block, W, C), lambda n: (n, 0, 0)),
                   pl.BlockSpec((1, C), lambda n: (0, 0)),
                   pl.BlockSpec((H, C), lambda n: (0, 0))],
-        out_specs=[pl.BlockSpec((H, copies, W, block), lambda n: (0, 0, 0, n)),
-                   pl.BlockSpec((W, C, block), lambda n: (0, 0, n)),
-                   pl.BlockSpec((W, block), lambda n: (0, n))],
-        out_shape=[jax.ShapeDtypeStruct((H, copies, W, I), BF16),
-                   jax.ShapeDtypeStruct((W, C, I), BF16),
-                   jax.ShapeDtypeStruct((W, I), F32)],
+        out_specs=pl.BlockSpec((H, copies, W, block), lambda n: (0, 0, 0, n)),
+        out_shape=jax.ShapeDtypeStruct((H, copies, W, I), BF16),
         scratch_shapes=[pltpu.VMEM((block * (W + 1), C), F32)],
-        compiler_params=pltpu.CompilerParams(vmem_limit_bytes=32 * 1024 * 1024),
+        compiler_params=pltpu.CompilerParams(vmem_limit_bytes=VMEM),
         cost_estimate=pl.CostEstimate(flops=20 << 30, bytes_accessed=40 << 20, transcendentals=0),
         name="pair_bias",
     )(pair, gain.reshape(1, C), weight.T)
+
+
+def hat_kernel(pair_ref, hat_ref, inv_ref, x_s):
+    for j, hat, inv in turned(pair_ref, x_s):
+        hat_ref[j] = hat.astype(BF16)
+        inv_ref[j:j + 1, :] = inv
+
+
+def pair_hat(pair, block=256):
+    I, W, C = pair.shape
+    return pl.pallas_call(
+        hat_kernel,
+        grid=(I // block,),
+        in_specs=[pl.BlockSpec((block, W, C), lambda n: (n, 0, 0))],
+        out_specs=[pl.BlockSpec((W, C, block), lambda n: (0, 0, n)),
+                   pl.BlockSpec((W, block), lambda n: (0, n))],
+        out_shape=[jax.ShapeDtypeStruct((W, C, I), BF16), jax.ShapeDtypeStruct((W, I), F32)],
+        scratch_shapes=[pltpu.VMEM((block * (W + 1), C), F32)],
+        compiler_params=pltpu.CompilerParams(vmem_limit_bytes=VMEM),
+        cost_estimate=pl.CostEstimate(flops=4 << 30, bytes_accessed=20 << 20, transcendentals=0),
+        name="pair_hat",
+    )(pair)
 
 
 def grad_kernel(part_ref, bias_ref, inv_ref, hat_ref, weight_ref, out_ref, y_s):
@@ -117,12 +141,6 @@
     )(parts, bias, inv, hat, weight)
 
 
-def grad_weight(weight, gain):
-    scaled = weight.astype(F32) * gain[:, None]
-    hi, lo = split((scaled - jnp.mean(scaled, axis=0, keepdims=True)).T)
-    return jnp.concatenate([spread(w.astype(F32)).astype(BF16) for w in (hi, hi, lo)], 0).T
-
-
 def attend_kernel(core_ref, mine_ref, other_ref, mask_ref, q_ref, k_ref, v_ref, g_ref,
                   o_ref, dq_ref, keep_ref, send_ref,
                   bias_s, acc_s, s0_s, s1_s, e0_s, e1_s, kt_s, vt_s, kc_s, g2_s, mask_s):
@@ -132,7 +150,8 @@
     dh = q_ref.shape[-2]
     n_j = bias_s.shape[0]
     rows = k_ref.shape[0]
-    per = JT = n_j // rows
+    per = n_j // rows
+    JT = 2 * per
     core = core_ref[0]
     blocks = mine_ref.shape[0]
     bj = mine_ref.shape[1]
@@ -147,7 +166,7 @@
 
     @pl.when(step == 0)
     def _():
-        mask_s[...] = jnp.concatenate([mask_ref[r, 0, :16, :].astype(F32) for r in range(rows)], 1).T
+        mask_s[...] = jnp.concatenate([mask_ref[r].astype(F32) for r in range(rows)], 1).T
 
         @pl.loop(0, blocks, unroll=4)
         def _(b):
@@ -180,15 +199,12 @@
 
     def soften(h, m):
         il = half[h]
-        o = None
-        one = jnp.ones((16, JT), BF16)
         for t in tiles:
-            e = jnp.exp2(s_s[h][t:t + JT, :] - m).astype(BF16)
-            e_s[h][t:t + JT, :] = e
-            v = v_ref[t // per, 0]
-            ot = jnp.dot(jnp.concatenate([v, one], 0), e, preferred_element_type=F32)
-            o = ot if o is None else o + ot
+            e_s[h][t:t + JT, :] = jnp.exp2(s_s[h][t:t + JT, :] - m).astype(BF16)
             yield None
+        v = jnp.concatenate([v_ref[r] for r in range(rows)], 1)
+        o = jnp.dot(jnp.concatenate([v, jnp.ones((16, n_j), BF16)], 0), e_s[h][...], preferred_element_type=F32)
+        yield None
         inv = 1.0 / o[dh:dh + 1, :]
         o = o[:dh] * inv
         o_ref[0, :, il] = o.astype(BF16)
@@ -230,14 +246,14 @@
 
     for r in range(rows):
         sl = slice(r * per, (r + 1) * per)
-        kz = k_ref[r, 0] * mask_ref[r, 0]
+        kz = k_ref[r] * mask_ref[r, 0:1, :]
         kt_s[sl, :] = jnp.concatenate([kz, kz], 0).T
     m0, _ = together(scores(0), backward(1, jnp.maximum(step - 1, 0), g2_s[...]))
     for r in range(rows):
         sl = slice(r * per, (r + 1) * per)
-        v = v_ref[r, 0]
+        v = v_ref[r]
         vt_s[sl, :] = jnp.concatenate([v, v, jnp.ones((16, per), BF16)], 0).T
-        kc_s[:, sl] = k_ref[r, 0]
+        kc_s[:, sl] = k_ref[r]
     g20, m1 = together(soften(0, m0), scores(1))
     _, g21 = together(backward(0, step, g20), soften(1, m1))
     g2_s[...] = g21
@@ -254,17 +270,17 @@
 
 def attention(core, mine, other, q, kv, g):
     S, dh, I = q.shape
-    R, per = kv.shape[0], kv.shape[3]
+    R, per = kv.shape[0], kv.shape[2]
     J = R * per
     IH = I // 2
     full = lambda a: pl.BlockSpec(a.shape, lambda s: (0,) * a.ndim)
     one = pl.BlockSpec((1, dh, I), lambda s: (s, 0, 0))
-    all_rows = lambda at: pl.BlockSpec((R, 1, dh, per), lambda s: (0, at(s), 0, 0))
+    all_rows = lambda n, at: pl.BlockSpec((R, n, per), lambda s: (0, at(s), 0))
     return pl.pallas_call(
         attend_kernel,
         grid=(S,),
-        in_specs=[pl.BlockSpec(memory_space=pltpu.SMEM), full(mine), full(other), all_rows(lambda s: 2 * S),
-                  one, all_rows(lambda s: s), all_rows(lambda s: s + S), one],
+        in_specs=[pl.BlockSpec(memory_space=pltpu.SMEM), full(mine), full(other), all_rows(MASK, lambda s: 2 * S * dh // MASK),
+                  one, all_rows(dh, lambda s: s), all_rows(dh, lambda s: s + S), one],
         out_specs=[one, full(q), full(mine), full(other)],
         out_shape=[jax.ShapeDtypeStruct(a.shape, BF16) for a in (q, q, mine, other)],
         scratch_shapes=[pltpu.VMEM((J, I), F32), pltpu.VMEM((J, I), F32),
@@ -273,27 +289,44 @@
                         pltpu.VMEM((J, 2 * dh), BF16), pltpu.VMEM((J, 2 * dh + 16), BF16),
                         pltpu.VMEM((dh, J), BF16), pltpu.VMEM((2 * dh + 16, IH), BF16),
                         pltpu.VMEM((J, 16), F32)],
-        compiler_params=pltpu.CompilerParams(vmem_limit_bytes=32 * 1024 * 1024),
+        compiler_params=pltpu.CompilerParams(vmem_limit_bytes=61 * 1024 * 1024),
+        input_output_aliases={1: 2, 2: 3},
         cost_estimate=pl.CostEstimate(flops=8 * S * J * I * dh, bytes_accessed=12 << 20, transcendentals=S * I * J),
         name="attend",
     )(core, mine, other, kv, q, kv, kv, g)
 
 
 def pack_kernel(k_ref, v_ref, m_ref, out_ref):
-    S = k_ref.shape[0]
-    out_ref[:S] = k_ref[...]
-    out_ref[S:2 * S] = v_ref[...]
-    out_ref[2 * S] = jnp.broadcast_to(m_ref[...].astype(F32), out_ref.shape[1:]).astype(BF16)
+    S, dh, per = k_ref.shape
+    out_ref[:S * dh] = k_ref[...].reshape(S * dh, per)
+    out_ref[S * dh:2 * S * dh] = v_ref[...].reshape(S * dh, per)
+    out_ref[2 * S * dh:] = jnp.broadcast_to(m_ref[...].astype(F32), (MASK, per)).astype(BF16)
 
 
 def pack(k, v, mask):
     S, dh, per = k.shape
     return pl.pallas_call(
         pack_kernel,
-        out_shape=jax.ShapeDtypeStruct((2 * S + 1, dh, per), BF16),
-        compiler_params=pltpu.CompilerParams(vmem_limit_bytes=8 * 1024 * 1024),
+        out_shape=jax.ShapeDtypeStruct((2 * S * dh + MASK, per), BF16),
+        compiler_params=pltpu.CompilerParams(vmem_limit_bytes=VMEM),
         name="pack",
     )(k, v, mask.reshape(1, per))
+
+
+def weight_kernel(weight_ref, gain_ref, out_ref):
+    scaled = weight_ref[...].astype(F32) * gain_ref[...]
+    hi, lo = (x.astype(F32) for x in split(scaled - jnp.mean(scaled, axis=1, keepdims=True)))
+    out_ref[...] = jnp.concatenate([spread(w) for w in (hi, hi, lo)], 0).T.astype(BF16)
+
+
+def grad_weight(weight, gain):
+    C, H = weight.shape
+    return pl.pallas_call(
+        weight_kernel,
+        out_shape=jax.ShapeDtypeStruct((GROUP * C, 3 * H * GROUP), BF16),
+        compiler_params=pltpu.CompilerParams(vmem_limit_bytes=32 * 1024 * 1024),
+        name="grad_weight",
+    )(weight.T, gain.reshape(1, C))
 
 
 def local(pair, pair_gain, pair_weight, queries, keys, values, d_atoms, key_mask, atom_token):
@@ -302,7 +335,7 @@
     spread_out = lambda x: lax.all_to_all(x, ("col", "zhi"), 0, 0, tiled=True)
 
     kv = lax.all_gather(pack(keys[:, 0], values[:, 0], key_mask), "row")
-    bias, hat, inv = pair_bias(pair, pair_gain, pair_weight, lax.axis_size("zhi"))
+    bias = pair_bias(pair, pair_gain, pair_weight, lax.axis_size("zhi"))
     heads, copies, width, _ = bias.shape
     mine = spread_out(bias.reshape(heads * copies, width, strip))
     other = swap(mine)
@@ -317,11 +350,14 @@
 
     core = lax.axis_index("core").astype(jnp.int32).reshape(1)
     weight = grad_weight(pair_weight, pair_gain)
-    kv, weight = lax.optimization_barrier((kv, weight))
+    kv, grad_out, weight = lax.optimization_barrier((kv, grad_out, weight))
     o, dq, keep, send = attention(core, mine, other, queries[:, 0], kv, grad_out)
 
     chip = (keep.astype(F32) + swap(send).astype(F32)).astype(BF16)
-    d_pair = pair_grad(spread_out(chip), bias, inv, hat, weight)
+    chip, pair = lax.optimization_barrier((chip, pair))
+    parts = spread_out(chip)
+    hat, inv = pair_hat(pair)
+    d_pair = pair_grad(parts, bias, inv, hat, weight)
     return (o[:, None], dq[:, None], d_pair)
 
 

time: 154 us -> 156 us (1.013)
  Pallas kernels: 44 us -> 54 us
  local copies, waits for them, and re-layouts: 11.2 us -> 5.08 us
  other arithmetic: 7.74 us -> 2.61 us
  blocking collectives: 36.2 us -> 39.8 us
  starting transfers between devices: 12.4 us -> 10.4 us
    pallas_call x1 -> x3, Pallas kernels: 1.04 us -> 9.13 us  [the longest x1 6.44 us: pair_hat(): pl.pallas_call(hat_kernel, grid=(I // block,), in_specs=[pl.BlockSpec((bl...]
    unnamed x32 -> x20, local copies, waits for them, and re-layouts: 10.9 us -> 5.08 us
    unnamed x13 -> x0, other arithmetic: 3.87 us -> none
    all_to_all x1, blocking collectives: 36.2 us -> 39.8 us  [local(): spread_out = lambda x: lax.all_to_all(x, ('col', 'zhi'), 0, 0, tiled=True)]
    all_gather x1, waiting for transfers between devices: 0.01 us -> 2.47 us  [local(): kv = lax.all_gather(pack(keys[:, 0], values[:, 0], key_mask), 'row')]
    convert_element_type x1, other arithmetic: 0.38 us -> 2.61 us  [local(): chip = (keep.astype(F32) + swap(send).astype(F32)).astype(BF16)]
    transpose x1 -> x0, other arithmetic: 1.95 us -> none  [grad_weight(): jnp.concatenate([spread(w.astype(F32)).astype(BF16) for w in (hi, hi, lo)...]
    all_to_all x1, waiting for transfers between devices: 23.5 us -> 21.7 us  [local(): spread_out = lambda x: lax.all_to_all(x, ('col', 'zhi'), 0, 0, tiled=True)]
  transfers between devices with their start and end apart: 4 -> 4, of which waited for: 2 -> 3; matrix products, arithmetic and copies ran while one was open for 6% -> 1% of each run, Pallas kernels for 3% -> 9%
where the time goes in v3:
time: 156 us; the launch traced here: 155 us
  Pallas kernels  54 us (35%)
  blocking collectives  39.8 us (26%)
  waiting for transfers between devices  27 us (17%)
  between operations  14.1 us (9%)
  starting transfers between devices  10.4 us (7%)
  local copies, waits for them, and re-layouts  5.08 us (3%)
  other arithmetic  2.61 us (2%)
  matrix products  2.22 us (1%)
    all_to_all x1, blocking collectives, local(): spread_out = lambda x: lax.all_to_all(x, ('col', 'zhi'), 0, 0, tiled=True)  39.8 us
    pallas_call x1, Pallas kernels, attention(): pl.pallas_call(attend_kernel, grid=(S,), in_specs=[pl.BlockSpec(memory_sp...  32.8 us
    all_to_all x1, waiting for transfers between devices, local(): spread_out = lambda x: lax.all_to_all(x, ('col', 'zhi'), 0, 0, tiled=True)  21.7 us
    all_to_all x1, starting transfers between devices, local(): spread_out = lambda x: lax.all_to_all(x, ('col', 'zhi'), 0, 0, tiled=True)  10.2 us
    pallas_call x1, Pallas kernels, pair_bias(): pl.pallas_call(bias_kernel, grid=(I // block,), in_specs=[pl.BlockSpec((b...  6.53 us
    pallas_call x1, Pallas kernels, pair_hat(): pl.pallas_call(hat_kernel, grid=(I // block,), in_specs=[pl.BlockSpec((bl...  6.44 us
    pallas_call x1, Pallas kernels, pair_grad(): pl.pallas_call(grad_kernel, grid=(I // block,), in_specs=[pl.BlockSpec((H...  5.59 us
    unnamed x20, local copies, waits for them, and re-layouts  5.08 us
  transfers between devices with their start and end apart: 4, of which 3 were waited for; matrix products, arithmetic and copies ran while one was open for 1% of the time, Pallas kernels for 9%

profile of v3, /device:TPU:8, one launch (start us, length us, event | category | flops | bytes accessed | tf_op | source)
XLA Modules:
  0.0 155.2 jit_solution(10214551623972397618)
XLA Ops:
  7.2 0.0 copy-start
  7.2 0.0 all-gather.3.cloned.1.call-start
  7.2 2.4 %pack.1 = bf16[976,512]{1,0:T(8,128)(2,1)} custom-call(bf16[10,48,512]{2,1,0:T(8,128)(2,1)} %bitcast.36, bf16[10,48,512]{2,1,0:T(8,128)(2,1)} %bitcast.37, s32[1,512]{1,0:T(1,128)} %bitcast.38), custom_call_target="tpu_custom_call" | custom-call | tf_op jit(solution)/shard_map/pack/pallas_call | solution.py:308
  9.6 0.0 all-gather.3.cloned.1.call-update
  9.6 6.5 %pair_bias.1.bias_ref = bf16[16,2,32,512]{3,2,1,0:T(8,128)(2,1)} custom-call(bf16[512,32,128]{2,1,0:T(8,128)(2,1)} %pair_ref.2, f32[1,128]{1,0:T(1,128)} %bitcast.34, bf16[16,128]{1,0:T(8,128)(2,1)} %bitcast.32), custom_call_target="tpu_custom_call" | custom-call | flops 21474836480 | bytes 41943040 | tf_op jit(solution)/shard_map/pair_bias/pallas_call | solution.py:65
  16.1 0.0 copy-start.4
  16.1 0.0 copy-start.5
  16.1 0.0 copy-start.9
  16.2 39.8 %all_to_all.10.mine_ref = bf16[32,32,512]{2,1,0:T(8,128)(2,1)S(1)} all-to-all(bf16[32,32,512]{2,1,0:T(8,128)(2,1)} %bitcast.31), channel_id=1, replica_groups=mesh['row'=4,'col'=16,'zhi'=2,'core'=2] {'col','zhi'}, dimensions={0} | all-to-all | bytes 2097152 | tf_op jit(solution)/shard_map/all_to_all | solution.py:335
  56.0 0.0 copy-start.8
  56.0 0.0 collective-permute-start
  56.0 0.0 copy-done.4
  56.0 0.0 copy-done.5
  56.0 0.3 grad_weight.1.weight_ref
  56.3 0.0 copy-start.2
  56.3 0.9 copy-done.2
  57.2 0.0 copy-done.9
  57.2 0.0 copy-done
  57.2 2.2 %fusion.10.g_ref = bf16[10,48,512]{2,1,0:T(8,128)(2,1)} fusion(bf16[10,1,48,2048]{3,2,1,0:T(8,128)(2,1)S(1)} %copy-done, s32[2048]{0:T(1024)S(1)} %broadcast_subtract_fusion), kind=kOutput, calls=%fused_computation.7 | convolution fusion | flops 1007927296 | bytes 2465792 | tf_op jit(solution)/shard_map/sda,at->sdt/dot_general | solution.py:347
  59.4 0.0 copy-done.8
  59.4 2.5 %all-gather.3.cloned.1.call-done = bf16[3904,512]{1,0:T(8,128)(2,1)} async-done(((bf16[976,512]{1,0:T(8,128)(2,1)}), bf16[3904,512]{1,0:T(8,128)(2,1)}) %all-gather.3.cloned.1.call-update) | async-done | bytes 3997712 | tf_op jit(solution)/shard_map/all_gather | solution.py:337
  61.9 0.0 collective-permute-done.other_ref
  61.9 32.8 %attend.1 = (bf16[10,48,512]{2,1,0:T(8,128)(2,1)}, bf16[10,48,512]{2,1,0:T(8,128)(2,1)}, bf16[32,32,512]{2,1,0:T(8,128)(2,1)}, bf16[32,32,512]{2,1,0:T(8,128)(2,1)}) custom-call(s32[1]{0:T(128)} %bitcast.core_ref, bf16[32,32,512]{2,1,0:T(8,128)(2,1)} %copy-done.8, ...), custom_call_target="tpu_custom_call", output_to_operand_aliasing={{2}: (1, {}), {3}: (2, {})} | custom-call | flops 4026531840 | bytes 12582912 | tf_op jit(solution)/shard_map/attend/pallas_call | solution.py:279
  94.7 0.1 collective-permute-start.1
  94.8 2.9 %collective-permute-done.1 = bf16[32,32,512]{2,1,0:T(8,128)(2,1)S(1)} collective-permute-done((bf16[32,32,512]{2,1,0:T(8,128)(2,1)}, bf16[32,32,512]{2,1,0:T(8,128)(2,1)S(1)}, u32[]{:S(2)}, u32[]{:S(2)}) %collective-permute-start.1) | collective-permute-done | bytes 1048608 | tf_op jit(solution)/shard_map/ppermute | solution.py:334
  97.6 2.6 %add_convert_fusion = bf16[32,32,512]{2,1,0:T(8,128)(2,1)} fusion(bf16[32,32,512]{2,1,0:T(8,128)(2,1)S(1)} %collective-permute-done.1, bf16[32,32,512]{2,1,0:T(8,128)(2,1)} %get-tuple-element.18), kind=kLoop, calls=%fused_computation.3 | loop fusion | flops 2097152 | bytes 3145728 | tf_op jit(solution)/shard_map/convert_element_type | solution.py:356
  100.2 10.2 %all-to-all-start.1 = ((bf16[32,32,512]{2,1,0:T(8,128)(2,1)}), bf16[32,32,512]{2,1,0:T(8,128)(2,1)}, u32[]{:S(2)}, u32[]{:S(2)}) async-start(bf16[32,32,512]{2,1,0:T(8,128)(2,1)} %add_convert_fusion), calls=%async_computation.1 | async-start | bytes 2097152 | tf_op jit(solution)/shard_map/all_to_all | solution.py:335
  110.5 0.0 copy-start.1
  110.5 6.4 %pair_hat.1 = (bf16[32,128,512]{2,1,0:T(8,128)(2,1)}, f32[32,512]{1,0:T(8,128)}) custom-call(bf16[512,32,128]{2,1,0:T(8,128)(2,1)} %pair_ref.2), custom_call_target="tpu_custom_call" | custom-call | flops 4294967296 | bytes 20971520 | tf_op jit(solution)/shard_map/pair_hat/pallas_call | solution.py:88
  116.9 21.7 %all-to-all-done.1.part_ref = bf16[32,32,512]{2,1,0:T(8,128)(2,1)} async-done(((bf16[32,32,512]{2,1,0:T(8,128)(2,1)}), bf16[32,32,512]{2,1,0:T(8,128)(2,1)}, u32[]{:S(2)}, u32[]{:S(2)}) %all-to-all-start.1) | async-done | bytes 1048608 | tf_op jit(solution)/shard_map/all_to_all | solution.py:335
  138.6 0.0 copy-done.1
  138.6 0.0 copy-start.3
  138.6 1.1 copy-done.3
  139.7 0.0 copy-start.6
  139.7 2.2 %copy-done.6 = bf16[32,128,512]{2,1,0:T(8,128)(2,1)S(1)} copy-done((bf16[32,128,512]{2,1,0:T(8,128)(2,1)S(1)}, bf16[32,128,512]{2,1,0:T(8,128)(2,1)}, u32[]{:S(2)}) %copy-start.6) | copy-done | bytes 4194328
  141.9 0.0 copy-start.7
  141.9 0.8 copy-done.7
  142.8 5.6 %pair_grad.1 = bf16[512,32,128]{2,1,0:T(8,128)(2,1)} custom-call(bf16[32,32,512]{2,1,0:T(8,128)(2,1)} %all-to-all-done.1.part_ref, bf16[16,2,32,512]{3,2,1,0:T(8,128)(2,1)S(1)} %copy-done.1, f32[32,512]{1,0:T(8,128)S(1)} %copy-done.7, bf16[32,128,512]{2,1,0:T(8,128)(2,1)S(1)} %copy-done.6, bf16[1024,384]{1,0:T(8,128)(2,1)S(1)} %copy-done.3), custom_call_target="tpu_custom_call" | custom-call | flops 10737418240 | bytes 20971520 | tf_op jit(solution)/shard_map/pair_grad/pallas_call | solution.py:127
  (1 shorter events, 0.0 us)
Async XLA Ops:
  7.2 50.0 %copy-start = (bf16[10,1,48,2048]{3,2,1,0:T(8,128)(2,1)S(1)}, bf16[10,1,48,2048]{3,2,1,0:T(8,128)(2,1)}, u32[]{:S(2)}) copy-start(bf16[10,1,48,2048]{3,2,1,0:T(8,128)(2,1)} %param.15) | copy-start | bytes 5898244
  7.2 54.7 %all-gather.3.cloned.1.call-start = ((), (), s32[]{:S(2)}) async-start(), calls=%async_computation.2 | async-start | bytes 4997120 | tf_op jit(solution)/shard_map/all_gather | solution.py:337
  16.1 39.8 %copy-start.4 = (bf16[128,16]{0,1:T(8,128)(2,1)S(1)}, bf16[128,16]{0,1:T(8,128)(2,1)}, u32[]{:S(2)}) copy-start(bf16[128,16]{0,1:T(8,128)(2,1)} %param.11) | copy-start | bytes 12292
  16.1 39.8 %copy-start.5 = (f32[128]{0:T(128)S(1)}, f32[128]{0:T(128)}, u32[]{:S(2)}) copy-start(f32[128]{0:T(128)} %param.10) | copy-start | bytes 1540
  16.1 41.0 %copy-start.9 = (s32[2048]{0:T(1024)S(1)}, s32[2048]{0:T(1024)}, u32[]{:S(2)}) copy-start(s32[2048]{0:T(1024)} %param.17) | copy-start | bytes 24580
  56.0 3.5 %copy-start.8 = (bf16[32,32,512]{2,1,0:T(8,128)(2,1)}, bf16[32,32,512]{2,1,0:T(8,128)(2,1)S(1)}, u32[]{:S(2)}) copy-start(bf16[32,32,512]{2,1,0:T(8,128)(2,1)S(1)} %all_to_all.10.mine_ref) | copy-start | bytes 3145732
  56.0 5.9 %collective-permute-start = (bf16[32,32,512]{2,1,0:T(8,128)(2,1)S(1)}, bf16[32,32,512]{2,1,0:T(8,128)(2,1)}, u32[]{:S(2)}, u32[]{:S(2)}) collective-permute-start(bf16[32,32,512]{2,1,0:T(8,128)(2,1)S(1)} %all_to_all.10.mine_ref), channel_id=1, source_target_pairs={{0,1},{1,0},{2,3},{3,2},{4,5},{5,4},{6,7},{7,6},{8,9},{9,8},{10,11... | collective-permute-start | bytes 3145736 | tf_op jit(solution)/shard_map/ppermute | solution.py:334
  56.3 0.9 copy-start.2
  94.7 3.0 %collective-permute-start.1 = (bf16[32,32,512]{2,1,0:T(8,128)(2,1)}, bf16[32,32,512]{2,1,0:T(8,128)(2,1)S(1)}, u32[]{:S(2)}, u32[]{:S(2)}) collective-permute-start(bf16[32,32,512]{2,1,0:T(8,128)(2,1)} %get-tuple-element.19), channel_id=1, source_target_pairs={{0,1},{1,0},{2,3},{3,2},{4,5},{5,4},{6,7},{7,6},{8,9},{9,8},{10,11... | collective-permute-start | bytes 3145736 | tf_op jit(solution)/shard_map/ppermute | solution.py:334
  100.2 38.4 %all-to-all-start.1 = ((bf16[32,32,512]{2,1,0:T(8,128)(2,1)}), bf16[32,32,512]{2,1,0:T(8,128)(2,1)}, u32[]{:S(2)}, u32[]{:S(2)}) async-start(bf16[32,32,512]{2,1,0:T(8,128)(2,1)} %add_convert_fusion), calls=%async_computation.1 | async-start | bytes 2097152 | tf_op jit(solution)/shard_map/all_to_all | solution.py:335
  110.5 28.2 %copy-start.1 = (bf16[16,2,32,512]{3,2,1,0:T(8,128)(2,1)S(1)}, bf16[16,2,32,512]{3,2,1,0:T(8,128)(2,1)}, u32[]{:S(2)}) copy-start(bf16[16,2,32,512]{3,2,1,0:T(8,128)(2,1)} %pair_bias.1.bias_ref) | copy-start | bytes 3145732
  138.6 1.1 copy-start.3
  139.7 2.2 %copy-start.6 = (bf16[32,128,512]{2,1,0:T(8,128)(2,1)S(1)}, bf16[32,128,512]{2,1,0:T(8,128)(2,1)}, u32[]{:S(2)}) copy-start(bf16[32,128,512]{2,1,0:T(8,128)(2,1)} %get-tuple-element.23.hat_ref) | copy-start | bytes 12582916
  141.9 0.8 copy-start.7
Sparse Core Ops, SparseCore 0:
  9.8 52.0 all-gather.2

commit v4 on v3

--- a/solution.py
+++ b/solution.py
@@ -1,3 +1,4 @@
+import functools
 import math
 
 import jax
@@ -72,7 +73,7 @@
         out_shape=jax.ShapeDtypeStruct((H, copies, W, I), BF16),
         scratch_shapes=[pltpu.VMEM((block * (W + 1), C), F32)],
         compiler_params=pltpu.CompilerParams(vmem_limit_bytes=VMEM),
-        cost_estimate=pl.CostEstimate(flops=20 << 30, bytes_accessed=40 << 20, transcendentals=0),
+        cost_estimate=pl.CostEstimate(flops=100 << 30, bytes_accessed=40 << 20, transcendentals=0),
         name="pair_bias",
     )(pair, gain.reshape(1, C), weight.T)
 
@@ -94,7 +95,7 @@
         out_shape=[jax.ShapeDtypeStruct((W, C, I), BF16), jax.ShapeDtypeStruct((W, I), F32)],
         scratch_shapes=[pltpu.VMEM((block * (W + 1), C), F32)],
         compiler_params=pltpu.CompilerParams(vmem_limit_bytes=VMEM),
-        cost_estimate=pl.CostEstimate(flops=4 << 30, bytes_accessed=20 << 20, transcendentals=0),
+        cost_estimate=pl.CostEstimate(flops=400 << 30, bytes_accessed=20 << 20, transcendentals=0),
         name="pair_hat",
     )(pair)
 
@@ -141,18 +142,24 @@
     )(parts, bias, inv, hat, weight)
 
 
-def attend_kernel(core_ref, mine_ref, other_ref, mask_ref, q_ref, k_ref, v_ref, g_ref,
-                  o_ref, dq_ref, keep_ref, send_ref,
-                  bias_s, acc_s, s0_s, s1_s, e0_s, e1_s, kt_s, vt_s, kc_s, g2_s, mask_s):
+def attend_kernel(rows, place_ref, mine_ref, other_ref, q_ref, g_ref, *refs):
+    k_refs, v_refs, mask_refs = refs[:rows], refs[rows:2 * rows], refs[2 * rows:3 * rows]
+    attend_body(place_ref, mine_ref, other_ref, q_ref, g_ref, k_refs, v_refs, mask_refs, *refs[3 * rows:])
+
+
+def attend_body(place_ref, mine_ref, other_ref, q_ref, g_ref, k_refs, v_refs, mask_refs,
+                o_ref, dq_ref, keep_ref, send_ref,
+                bias_s, acc_s, s0_s, s1_s, e0_s, e1_s, kt_s, vt_s, kc_s, g2_s, mask_s):
     step = pl.program_id(0)
     steps = pl.num_programs(0)
     n_i = q_ref.shape[-1]
     dh = q_ref.shape[-2]
     n_j = bias_s.shape[0]
-    rows = k_ref.shape[0]
+    rows = len(k_refs)
     per = n_j // rows
     JT = 2 * per
-    core = core_ref[0]
+    core = place_ref[0]
+    row = place_ref[1]
     blocks = mine_ref.shape[0]
     bj = mine_ref.shape[1]
     scaling = 1.0 / math.sqrt(dh)
@@ -162,11 +169,13 @@
     e_s = (e0_s, e1_s)
 
     def position(b, parity):
-        return pl.ds(pl.multiple_of((b * 2 + parity) * bj, bj), bj)
+        token = (b * 2 + parity) * bj
+        token = (token // per + rows - row) % rows * per + token % per
+        return pl.ds(pl.multiple_of(token, bj), bj)
 
     @pl.when(step == 0)
     def _():
-        mask_s[...] = jnp.concatenate([mask_ref[r].astype(F32) for r in range(rows)], 1).T
+        mask_s[...] = jnp.concatenate([mask_refs[r][...].astype(F32) for r in range(rows)], 1).T
 
         @pl.loop(0, blocks, unroll=4)
         def _(b):
@@ -202,7 +211,7 @@
         for t in tiles:
             e_s[h][t:t + JT, :] = jnp.exp2(s_s[h][t:t + JT, :] - m).astype(BF16)
             yield None
-        v = jnp.concatenate([v_ref[r] for r in range(rows)], 1)
+        v = jnp.concatenate([v_refs[r][...] for r in range(rows)], 1)
         o = jnp.dot(jnp.concatenate([v, jnp.ones((16, n_j), BF16)], 0), e_s[h][...], preferred_element_type=F32)
         yield None
         inv = 1.0 / o[dh:dh + 1, :]
@@ -246,14 +255,14 @@
 
     for r in range(rows):
         sl = slice(r * per, (r + 1) * per)
-        kz = k_ref[r] * mask_ref[r, 0:1, :]
+        kz = k_refs[r][...] * mask_refs[r][0:1, :]
         kt_s[sl, :] = jnp.concatenate([kz, kz], 0).T
     m0, _ = together(scores(0), backward(1, jnp.maximum(step - 1, 0), g2_s[...]))
     for r in range(rows):
         sl = slice(r * per, (r + 1) * per)
-        v = v_ref[r]
+        v = v_refs[r][...]
         vt_s[sl, :] = jnp.concatenate([v, v, jnp.ones((16, per), BF16)], 0).T
-        kc_s[:, sl] = k_ref[r]
+        kc_s[:, sl] = k_refs[r][...]
     g20, m1 = together(soften(0, m0), scores(1))
     _, g21 = together(backward(0, step, g20), soften(1, m1))
     g2_s[...] = g21
@@ -268,19 +277,20 @@
                 dst[b] = acc_s[position(b, par), :].astype(BF16)
 
 
-def attention(core, mine, other, q, kv, g):
+def attention(place, mine, other, q, ks, vs, g):
     S, dh, I = q.shape
-    R, per = kv.shape[0], kv.shape[2]
+    R, per = len(ks), ks[0].shape[1]
     J = R * per
     IH = I // 2
     full = lambda a: pl.BlockSpec(a.shape, lambda s: (0,) * a.ndim)
     one = pl.BlockSpec((1, dh, I), lambda s: (s, 0, 0))
-    all_rows = lambda n, at: pl.BlockSpec((R, n, per), lambda s: (0, at(s), 0))
-    return pl.pallas_call(
-        attend_kernel,
+    own = pl.BlockSpec((dh, per), lambda s: (s, 0))
+    flags = pl.BlockSpec((MASK, per), lambda s: (S * dh // MASK, 0))
+    return pl.pallas_call(
+        functools.partial(attend_kernel, R),
         grid=(S,),
-        in_specs=[pl.BlockSpec(memory_space=pltpu.SMEM), full(mine), full(other), all_rows(MASK, lambda s: 2 * S * dh // MASK),
-                  one, all_rows(dh, lambda s: s), all_rows(dh, lambda s: s + S), one],
+        in_specs=[pl.BlockSpec(memory_space=pltpu.SMEM), full(mine), full(other), one, one]
+        + [own] * (2 * R) + [flags] * R,
         out_specs=[one, full(q), full(mine), full(other)],
         out_shape=[jax.ShapeDtypeStruct(a.shape, BF16) for a in (q, q, mine, other)],
         scratch_shapes=[pltpu.VMEM((J, I), F32), pltpu.VMEM((J, I), F32),
@@ -289,28 +299,27 @@
                         pltpu.VMEM((J, 2 * dh), BF16), pltpu.VMEM((J, 2 * dh + 16), BF16),
                         pltpu.VMEM((dh, J), BF16), pltpu.VMEM((2 * dh + 16, IH), BF16),
                         pltpu.VMEM((J, 16), F32)],
-        compiler_params=pltpu.CompilerParams(vmem_limit_bytes=61 * 1024 * 1024),
+        compiler_params=pltpu.CompilerParams(vmem_limit_bytes=121 * 512 * 1024),
         input_output_aliases={1: 2, 2: 3},
         cost_estimate=pl.CostEstimate(flops=8 * S * J * I * dh, bytes_accessed=12 << 20, transcendentals=S * I * J),
         name="attend",
-    )(core, mine, other, kv, q, kv, kv, g)
-
-
-def pack_kernel(k_ref, v_ref, m_ref, out_ref):
-    S, dh, per = k_ref.shape
-    out_ref[:S * dh] = k_ref[...].reshape(S * dh, per)
-    out_ref[S * dh:2 * S * dh] = v_ref[...].reshape(S * dh, per)
-    out_ref[2 * S * dh:] = jnp.broadcast_to(m_ref[...].astype(F32), (MASK, per)).astype(BF16)
-
-
-def pack(k, v, mask):
-    S, dh, per = k.shape
+    )(place, mine, other, q, g, *ks, *vs, *vs)
+
+
+def pack_kernel(v_ref, m_ref, out_ref):
+    S, dh, per = v_ref.shape
+    out_ref[:S * dh] = v_ref[...].reshape(S * dh, per)
+    out_ref[S * dh:] = jnp.broadcast_to(m_ref[...].astype(F32), (MASK, per)).astype(BF16)
+
+
+def pack(v, mask):
+    S, dh, per = v.shape
     return pl.pallas_call(
         pack_kernel,
-        out_shape=jax.ShapeDtypeStruct((2 * S * dh + MASK, per), BF16),
+        out_shape=jax.ShapeDtypeStruct((S * dh + MASK, per), BF16),
         compiler_params=pltpu.CompilerParams(vmem_limit_bytes=VMEM),
         name="pack",
-    )(k, v, mask.reshape(1, per))
+    )(v, mask.reshape(1, per))
 
 
 def weight_kernel(weight_ref, gain_ref, out_ref):
@@ -334,11 +343,21 @@
     swap = lambda x: lax.ppermute(x, "core", [(0, 1), (1, 0)])
     spread_out = lambda x: lax.all_to_all(x, ("col", "zhi"), 0, 0, tiled=True)
 
-    kv = lax.all_gather(pack(keys[:, 0], values[:, 0], key_mask), "row")
+    rows = lax.axis_size("row")
+    pass_on = lambda x, n: lax.ppermute(x, "row", [(i, (i + n) % rows) for i in range(rows)])
+    k = keys.reshape(-1, strip)
+    v = pack(values[:, 0], key_mask)
+    k_behind, v_ahead = pass_on(k, 1), pass_on(v, -1)
+    k_ahead, v_behind = pass_on(k, -1), pass_on(v, 1)
+    k_behind, v_ahead, again = lax.optimization_barrier((k_behind, v_ahead, pair))
+    hat, inv = pair_hat(again)
+    k_behind, v_ahead, hat, inv = lax.optimization_barrier((k_behind, v_ahead, hat, inv))
+    ks = [k, k_ahead, pass_on(k_behind, 1), k_behind]
+    vs = [v, v_ahead, pass_on(v_ahead, -1), v_behind]
+
     bias = pair_bias(pair, pair_gain, pair_weight, lax.axis_size("zhi"))
     heads, copies, width, _ = bias.shape
     mine = spread_out(bias.reshape(heads * copies, width, strip))
-    other = swap(mine)
 
     offset = lax.axis_index("row") * strip
     onehot = (
@@ -347,17 +366,15 @@
     grad_out = jnp.einsum(
         "sda,at->sdt", d_atoms[:, 0], onehot, preferred_element_type=F32
     ).astype(BF16)
-
-    core = lax.axis_index("core").astype(jnp.int32).reshape(1)
     weight = grad_weight(pair_weight, pair_gain)
-    kv, grad_out, weight = lax.optimization_barrier((kv, grad_out, weight))
-    o, dq, keep, send = attention(core, mine, other, queries[:, 0], kv, grad_out)
+    mine, ks, vs, grad_out, weight, hat, inv = lax.optimization_barrier(
+        (mine, ks, vs, grad_out, weight, hat, inv))
+    other = swap(mine)
+    place = jnp.stack([lax.axis_index("core"), lax.axis_index("row")]).astype(jnp.int32)
+    o, dq, keep, send = attention(place, mine, other, queries[:, 0], ks, vs, grad_out)
 
     chip = (keep.astype(F32) + swap(send).astype(F32)).astype(BF16)
-    chip, pair = lax.optimization_barrier((chip, pair))
-    parts = spread_out(chip)
-    hat, inv = pair_hat(pair)
-    d_pair = pair_grad(parts, bias, inv, hat, weight)
+    d_pair = pair_grad(spread_out(chip), bias, inv, hat, weight)
     return (o[:, None], dq[:, None], d_pair)
 
 

time: 156 us -> 135 us (0.87)
  between operations: 14.1 us -> 0.77 us
  starting transfers between devices: 10.4 us -> 21.8 us
  waiting for transfers between devices: 27 us -> 19.3 us
  blocking collectives: 39.8 us -> 33.8 us
  local copies, waits for them, and re-layouts: 5.08 us -> 0.05 us
    all_to_all x1, waiting for transfers between devices: 21.7 us -> 7.15 us  [local(): spread_out = lambda x: lax.all_to_all(x, ('col', 'zhi'), 0, 0, tiled=True)]
    ppermute x0 -> x6, starting transfers between devices: none -> 9.86 us  [local(): lax.ppermute(x, 'row', [(i, (i + n) % rows) for i in range(rows)])]
    ppermute x0 -> x6, waiting for transfers between devices: none -> 7.06 us  [local(): lax.ppermute(x, 'row', [(i, (i + n) % rows) for i in range(rows)])]
    all_to_all x1, blocking collectives: 39.8 us -> 33.8 us  [local(): spread_out = lambda x: lax.all_to_all(x, ('col', 'zhi'), 0, 0, tiled=True)]
    unnamed x20, local copies, waits for them, and re-layouts: 5.08 us -> 0.05 us
    all_gather x1 -> x0, waiting for transfers between devices: 2.47 us -> none  [local(): kv = lax.all_gather(pack(keys[:, 0], values[:, 0], key_mask), 'row')]
    ppermute x2, waiting for transfers between devices: 2.86 us -> 5.07 us  [local(): swap = lambda x: lax.ppermute(x, 'core', [(0, 1), (1, 0)])]
  transfers between devices with their start and end apart: 4 -> 9, of which waited for: 3 -> 4; matrix products, arithmetic and copies ran while one was open for 1% -> 2% of each run, Pallas kernels for 9% -> 11%
where the time goes in v4:
time: 135 us; the launch traced here: 134 us
  Pallas kernels  54.1 us (40%)
  blocking collectives  33.8 us (25%)
  starting transfers between devices  21.8 us (16%)
  waiting for transfers between devices  19.3 us (14%)
  other arithmetic  2.41 us (2%)
  matrix products  2.18 us (2%)
    all_to_all x1, blocking collectives, local(): spread_out = lambda x: lax.all_to_all(x, ('col', 'zhi'), 0, 0, tiled=True)  33.8 us
    pallas_call x1, Pallas kernels, attention(): pl.pallas_call(functools.partial(attend_kernel, R), grid=(S,), in_specs=[...  33.7 us
    all_to_all x1, starting transfers between devices, local(): spread_out = lambda x: lax.all_to_all(x, ('col', 'zhi'), 0, 0, tiled=True)  11.8 us
    ppermute x6, starting transfers between devices, local(): lax.ppermute(x, 'row', [(i, (i + n) % rows) for i in range(rows)])  9.86 us
    all_to_all x1, waiting for transfers between devices, local(): spread_out = lambda x: lax.all_to_all(x, ('col', 'zhi'), 0, 0, tiled=True)  7.15 us
    ppermute x6, waiting for transfers between devices, local(): lax.ppermute(x, 'row', [(i, (i + n) % rows) for i in range(rows)])  7.06 us
    pallas_call x1, Pallas kernels, pair_hat(): pl.pallas_call(hat_kernel, grid=(I // block,), in_specs=[pl.BlockSpec((bl...  6.71 us
    pallas_call x1, Pallas kernels, pair_bias(): pl.pallas_call(bias_kernel, grid=(I // block,), in_specs=[pl.BlockSpec((b...  6.55 us
  transfers between devices with their start and end apart: 9, of which 4 were waited for; matrix products, arithmetic and copies ran while one was open for 2% of the time, Pallas kernels for 11%

profile of v4, /device:TPU:8, one launch (start us, length us, event | category | flops | bytes accessed | tf_op | source)
XLA Modules:
  0.0 134.5 jit_solution(4213710495789483812)
XLA Ops:
  0.6 0.0 copy-start
  0.6 1.6 %collective-permute-start.1 = (bf16[480,512]{1,0:T(8,128)(2,1)}, bf16[480,512]{1,0:T(8,128)(2,1)S(1)}, u32[]{:S(2)}, u32[]{:S(2)}) collective-permute-start(bf16[480,512]{1,0:T(8,128)(2,1)} %bitcast.39), channel_id=1, source_target_pairs={{0,64},{64,128},{128,192},{192,0},{1,65},{65,129},{129,193},{193,1... | collective-permute-start | bytes 1474568 | tf_op jit(solution)/shard_map/ppermute | solution.py:347
  2.2 1.7 %collective-permute-start = (bf16[480,512]{1,0:T(8,128)(2,1)}, bf16[480,512]{1,0:T(8,128)(2,1)}, u32[]{:S(2)}, u32[]{:S(2)}) collective-permute-start(bf16[480,512]{1,0:T(8,128)(2,1)} %bitcast.40), channel_id=1, source_target_pairs={{0,192},{64,0},{128,64},{192,128},{1,193},{65,1},{129,65},{193,129... | collective-permute-start | bytes 1474568 | tf_op jit(solution)/shard_map/ppermute | solution.py:347
  4.0 1.9 %pack.1.refs_4_.refs_8_ = bf16[496,512]{1,0:T(8,128)(2,1)} custom-call(bf16[10,48,512]{2,1,0:T(8,128)(2,1)} %bitcast.36, s32[1,512]{1,0:T(1,128)} %bitcast.37), custom_call_target="tpu_custom_call" | custom-call | tf_op jit(solution)/shard_map/pack/pallas_call | solution.py:317
  5.8 0.3 collective-permute-start.5
  6.1 3.0 %collective-permute-start.2 = (bf16[496,512]{1,0:T(8,128)(2,1)}, bf16[496,512]{1,0:T(8,128)(2,1)S(1)}, u32[]{:S(2)}, u32[]{:S(2)}) collective-permute-start(bf16[496,512]{1,0:T(8,128)(2,1)} %pack.1.refs_4_.refs_8_), channel_id=1, source_target_pairs={{0,192},{64,0},{128,64},{192,128},{1,193},{65,1},{129,65},{193,129... | collective-permute-start | bytes 1523720 | tf_op jit(solution)/shard_map/ppermute | solution.py:347
  9.1 6.5 %pair_bias.1.bias_ref = bf16[16,2,32,512]{3,2,1,0:T(8,128)(2,1)} custom-call(bf16[512,32,128]{2,1,0:T(8,128)(2,1)} %pair_ref.2, f32[1,128]{1,0:T(1,128)} %bitcast.34, bf16[16,128]{1,0:T(8,128)(2,1)} %bitcast.32), custom_call_target="tpu_custom_call" | custom-call | flops 107374182400 | bytes 41943040 | tf_op jit(solution)/shard_map/pair_bias/pallas_call | solution.py:66
  15.6 11.8 %all-to-all-start = ((bf16[32,32,512]{2,1,0:T(8,128)(2,1)}), bf16[32,32,512]{2,1,0:T(8,128)(2,1)}, u32[]{:S(2)}, u32[]{:S(2)}) async-start(bf16[32,32,512]{2,1,0:T(8,128)(2,1)} %bitcast.31), calls=%async_computation | async-start | bytes 2097152 | tf_op jit(solution)/shard_map/all_to_all | solution.py:344
  27.4 0.0 collective-permute-done.1.refs_3_
  27.4 0.0 copy-start.9
  27.4 0.0 collective-permute-done.2.refs_5_.refs_9_
  27.4 0.0 copy-start.7
  27.4 0.0 copy-start.6
  27.4 0.0 copy-start.2
  27.4 0.0 copy-start.3
  27.4 6.7 %pair_hat.1 = (bf16[32,128,512]{2,1,0:T(8,128)(2,1)}, f32[32,512]{1,0:T(8,128)}) custom-call(bf16[512,32,128]{2,1,0:T(8,128)(2,1)} %pair_ref.2), custom_call_target="tpu_custom_call" | custom-call | flops 429496729600 | bytes 20971520 | tf_op jit(solution)/shard_map/pair_hat/pallas_call | solution.py:89
  34.1 0.0 copy-done.9
  34.2 0.0 copy-done.7
  34.2 0.1 collective-permute-start.3
  34.2 3.2 %collective-permute-start.4 = (bf16[496,512]{1,0:T(8,128)(2,1)}, bf16[496,512]{1,0:T(8,128)(2,1)S(1)}, u32[]{:S(2)}, u32[]{:S(2)}) collective-permute-start(bf16[496,512]{1,0:T(8,128)(2,1)} %copy-done.7), channel_id=1, source_target_pairs={{0,192},{64,0},{128,64},{192,128},{1,193},{65,1},{129,65},{193,129... | collective-permute-start | bytes 1523720 | tf_op jit(solution)/shard_map/ppermute | solution.py:347
  37.5 0.0 copy-done.6
  37.5 0.0 copy-done.2
  37.5 0.0 copy-done.3
  37.5 0.3 grad_weight.1.weight_ref
  37.8 0.0 copy-done
  37.8 2.2 %fusion.10.g_ref = bf16[10,48,512]{2,1,0:T(8,128)(2,1)} fusion(bf16[10,1,48,2048]{3,2,1,0:T(8,128)(2,1)S(1)} %copy-done, s32[2048]{0:T(1024)S(1)} %broadcast_subtract_fusion), kind=kOutput, calls=%fused_computation.7 | convolution fusion | flops 1007927296 | bytes 2465792 | tf_op jit(solution)/shard_map/sda,at->sdt/dot_general | solution.py:366
  40.0 0.0 collective-permute-done.refs_1_
  40.0 0.0 collective-permute-done.5.refs_7_.refs_11_
  40.0 7.0 %collective-permute-done.3.refs_2_ = bf16[480,512]{1,0:T(8,128)(2,1)} collective-permute-done((bf16[480,512]{1,0:T(8,128)(2,1)}, bf16[480,512]{1,0:T(8,128)(2,1)}, u32[]{:S(2)}, u32[]{:S(2)}) %collective-permute-start.3) | collective-permute-done | bytes 491552 | tf_op jit(solution)/shard_map/ppermute | solution.py:347
  47.0 0.0 collective-permute-done.4.refs_6_.refs_10_
  47.1 0.0 copy-start.8
  47.1 7.2 %all-to-all-done.mine_ref = bf16[32,32,512]{2,1,0:T(8,128)(2,1)} async-done(((bf16[32,32,512]{2,1,0:T(8,128)(2,1)}), bf16[32,32,512]{2,1,0:T(8,128)(2,1)}, u32[]{:S(2)}, u32[]{:S(2)}) %all-to-all-start) | async-done | bytes 1048608 | tf_op jit(solution)/shard_map/all_to_all | solution.py:344
  54.2 0.0 collective-permute-start.6
  54.2 0.7 pad_add_fusion.place_ref
  54.9 2.3 %collective-permute-done.6.other_ref = bf16[32,32,512]{2,1,0:T(8,128)(2,1)} collective-permute-done((bf16[32,32,512]{2,1,0:T(8,128)(2,1)}, bf16[32,32,512]{2,1,0:T(8,128)(2,1)}, u32[]{:S(2)}, u32[]{:S(2)}) %collective-permute-start.6) | collective-permute-done | bytes 1048608 | tf_op jit(solution)/shard_map/ppermute | solution.py:343
  57.2 0.0 copy-done.8
  57.2 0.0 copy-start.5
  57.2 33.7 %attend.1 = (bf16[10,48,512]{2,1,0:T(8,128)(2,1)}, bf16[10,48,512]{2,1,0:T(8,128)(2,1)}, bf16[32,32,512]{2,1,0:T(8,128)(2,1)}, bf16[32,32,512]{2,1,0:T(8,128)(2,1)}) custom-call(s32[2]{0:T(128)} %pad_add_fusion.place_ref, bf16[32,32,512]{2,1,0:T(8,128)(2,1)} %all-to-all-done.mine_ref, ...), custom_call_target="tpu_custom_call", output_to_operand_aliasing={{2}: (1, {}), {3}: (2, {})} | custom-call | flops 4026531840 | bytes 12582912 | tf_op jit(solution)/shard_map/attend/pallas_call | solution.py:289
  91.0 0.2 collective-permute-start.7
  91.2 2.7 %collective-permute-done.7 = bf16[32,32,512]{2,1,0:T(8,128)(2,1)S(1)} collective-permute-done((bf16[32,32,512]{2,1,0:T(8,128)(2,1)}, bf16[32,32,512]{2,1,0:T(8,128)(2,1)S(1)}, u32[]{:S(2)}, u32[]{:S(2)}) %collective-permute-start.7) | collective-permute-done | bytes 1048608 | tf_op jit(solution)/shard_map/ppermute | solution.py:343
  93.9 0.0 copy-start.1
  93.9 0.0 copy-start.4
  93.9 1.7 %add_convert_fusion = bf16[32,32,512]{2,1,0:T(8,128)(2,1)S(1)} fusion(bf16[32,32,512]{2,1,0:T(8,128)(2,1)S(1)} %collective-permute-done.7, bf16[32,32,512]{2,1,0:T(8,128)(2,1)} %get-tuple-element.50), kind=kLoop, calls=%fused_computation.3 | loop fusion | flops 2097152 | bytes 3145728 | tf_op jit(solution)/shard_map/convert_element_type | solution.py:376
  95.7 33.8 %all_to_all.10.part_ref = bf16[32,32,512]{2,1,0:T(8,128)(2,1)S(1)} all-to-all(bf16[32,32,512]{2,1,0:T(8,128)(2,1)S(1)} %add_convert_fusion), channel_id=1, replica_groups=mesh['row'=4,'col'=16,'zhi'=2,'core'=2] {'col','zhi'}, dimensions={0} | all-to-all | bytes 2097152 | tf_op jit(solution)/shard_map/all_to_all | solution.py:344
  129.5 0.0 copy-done.5
  129.5 0.0 copy-done.1
  129.5 0.0 copy-done.4
  129.5 5.0 %pair_grad.1 = bf16[512,32,128]{2,1,0:T(8,128)(2,1)} custom-call(bf16[32,32,512]{2,1,0:T(8,128)(2,1)S(1)} %all_to_all.10.part_ref, bf16[16,2,32,512]{3,2,1,0:T(8,128)(2,1)S(1)} %copy-done.1, f32[32,512]{1,0:T(8,128)S(1)} %copy-done.5, bf16[32,128,512]{2,1,0:T(8,128)(2,1)S(1)} %copy-done.4, bf16[1024,384]{1,0:T(8,128)(2,1)S(1)} %grad_weight.1.weight_ref), custom_call_target="tpu_custom_call" | custom-call | flops 10737418240 | bytes 20971520 | tf_op jit(solution)/shard_map/pair_grad/pallas_call | solution.py:128
  (1 shorter events, 0.0 us)
Async XLA Ops:
  0.6 37.2 %copy-start = (bf16[10,1,48,2048]{3,2,1,0:T(8,128)(2,1)S(1)}, bf16[10,1,48,2048]{3,2,1,0:T(8,128)(2,1)}, u32[]{:S(2)}) copy-start(bf16[10,1,48,2048]{3,2,1,0:T(8,128)(2,1)} %param.15) | copy-start | bytes 5898244
  0.6 26.7 %collective-permute-start.1 = (bf16[480,512]{1,0:T(8,128)(2,1)}, bf16[480,512]{1,0:T(8,128)(2,1)S(1)}, u32[]{:S(2)}, u32[]{:S(2)}) collective-permute-start(bf16[480,512]{1,0:T(8,128)(2,1)} %bitcast.39), channel_id=1, source_target_pairs={{0,64},{64,128},{128,192},{192,0},{1,65},{65,129},{129,193},{193,1... | collective-permute-start | bytes 1474568 | tf_op jit(solution)/shard_map/ppermute | solution.py:347
  2.2 37.8 %collective-permute-start = (bf16[480,512]{1,0:T(8,128)(2,1)}, bf16[480,512]{1,0:T(8,128)(2,1)}, u32[]{:S(2)}, u32[]{:S(2)}) collective-permute-start(bf16[480,512]{1,0:T(8,128)(2,1)} %bitcast.40), channel_id=1, source_target_pairs={{0,192},{64,0},{128,64},{192,128},{1,193},{65,1},{129,65},{193,129... | collective-permute-start | bytes 1474568 | tf_op jit(solution)/shard_map/ppermute | solution.py:347
  5.8 34.2 %collective-permute-start.5 = (bf16[496,512]{1,0:T(8,128)(2,1)}, bf16[496,512]{1,0:T(8,128)(2,1)}, u32[]{:S(2)}, u32[]{:S(2)}) collective-permute-start(bf16[496,512]{1,0:T(8,128)(2,1)} %pack.1.refs_4_.refs_8_), channel_id=1, source_target_pairs={{0,64},{64,128},{128,192},{192,0},{1,65},{65,129},{129,193},{193,1... | collective-permute-start | bytes 1523720 | tf_op jit(solution)/shard_map/ppermute | solution.py:347
  6.1 21.3 %collective-permute-start.2 = (bf16[496,512]{1,0:T(8,128)(2,1)}, bf16[496,512]{1,0:T(8,128)(2,1)S(1)}, u32[]{:S(2)}, u32[]{:S(2)}) collective-permute-start(bf16[496,512]{1,0:T(8,128)(2,1)} %pack.1.refs_4_.refs_8_), channel_id=1, source_target_pairs={{0,192},{64,0},{128,64},{192,128},{1,193},{65,1},{129,65},{193,129... | collective-permute-start | bytes 1523720 | tf_op jit(solution)/shard_map/ppermute | solution.py:347
  15.6 38.6 %all-to-all-start = ((bf16[32,32,512]{2,1,0:T(8,128)(2,1)}), bf16[32,32,512]{2,1,0:T(8,128)(2,1)}, u32[]{:S(2)}, u32[]{:S(2)}) async-start(bf16[32,32,512]{2,1,0:T(8,128)(2,1)} %bitcast.31), calls=%async_computation | async-start | bytes 2097152 | tf_op jit(solution)/shard_map/all_to_all | solution.py:344
  27.4 6.8 %copy-start.9 = (bf16[480,512]{1,0:T(8,128)(2,1)}, bf16[480,512]{1,0:T(8,128)(2,1)S(1)}, u32[]{:S(2)}) copy-start(bf16[480,512]{1,0:T(8,128)(2,1)S(1)} %collective-permute-done.1.refs_3_) | copy-start | bytes 1474564
  27.4 6.8 %copy-start.7 = (bf16[496,512]{1,0:T(8,128)(2,1)}, bf16[496,512]{1,0:T(8,128)(2,1)S(1)}, u32[]{:S(2)}) copy-start(bf16[496,512]{1,0:T(8,128)(2,1)S(1)} %collective-permute-done.2.refs_5_.refs_9_) | copy-start | bytes 1523716
  27.4 10.1 %copy-start.6 = (s32[2048]{0:T(1024)S(1)}, s32[2048]{0:T(1024)}, u32[]{:S(2)}) copy-start(s32[2048]{0:T(1024)} %param.17) | copy-start | bytes 24580
  27.4 10.1 %copy-start.2 = (bf16[128,16]{0,1:T(8,128)(2,1)S(1)}, bf16[128,16]{0,1:T(8,128)(2,1)}, u32[]{:S(2)}) copy-start(bf16[128,16]{0,1:T(8,128)(2,1)} %param.11) | copy-start | bytes 12292
  27.4 10.1 %copy-start.3 = (f32[128]{0:T(128)S(1)}, f32[128]{0:T(128)}, u32[]{:S(2)}) copy-start(f32[128]{0:T(128)} %param.10) | copy-start | bytes 1540
  34.2 12.9 %collective-permute-start.3 = (bf16[480,512]{1,0:T(8,128)(2,1)}, bf16[480,512]{1,0:T(8,128)(2,1)}, u32[]{:S(2)}, u32[]{:S(2)}) collective-permute-start(bf16[480,512]{1,0:T(8,128)(2,1)} %copy-done.9), channel_id=1, source_target_pairs={{0,64},{64,128},{128,192},{192,0},{1,65},{65,129},{129,193},{193,1... | collective-permute-start | bytes 1474568 | tf_op jit(solution)/shard_map/ppermute | solution.py:347
  34.2 12.8 %collective-permute-start.4 = (bf16[496,512]{1,0:T(8,128)(2,1)}, bf16[496,512]{1,0:T(8,128)(2,1)S(1)}, u32[]{:S(2)}, u32[]{:S(2)}) collective-permute-start(bf16[496,512]{1,0:T(8,128)(2,1)} %copy-done.7), channel_id=1, source_target_pairs={{0,192},{64,0},{128,64},{192,128},{1,193},{65,1},{129,65},{193,129... | collective-permute-start | bytes 1523720 | tf_op jit(solution)/shard_map/ppermute | solution.py:347
  47.1 10.2 %copy-start.8 = (bf16[496,512]{1,0:T(8,128)(2,1)}, bf16[496,512]{1,0:T(8,128)(2,1)S(1)}, u32[]{:S(2)}) copy-start(bf16[496,512]{1,0:T(8,128)(2,1)S(1)} %collective-permute-done.4.refs_6_.refs_10_) | copy-start | bytes 1523716
  54.2 3.0 %collective-permute-start.6 = (bf16[32,32,512]{2,1,0:T(8,128)(2,1)}, bf16[32,32,512]{2,1,0:T(8,128)(2,1)}, u32[]{:S(2)}, u32[]{:S(2)}) collective-permute-start(bf16[32,32,512]{2,1,0:T(8,128)(2,1)} %all-to-all-done.mine_ref), channel_id=1, source_target_pairs={{0,1},{1,0},{2,3},{3,2},{4,5},{5,4},{6,7},{7,6},{8,9},{9,8},{10,11... | collective-permute-start | bytes 3145736 | tf_op jit(solution)/shard_map/ppermute | solution.py:343
  57.2 72.3 %copy-start.5 = (f32[32,512]{1,0:T(8,128)S(1)}, f32[32,512]{1,0:T(8,128)}, u32[]{:S(2)}) copy-start(f32[32,512]{1,0:T(8,128)} %get-tuple-element.52.inv_ref) | copy-start | bytes 196612
  91.0 3.0 %collective-permute-start.7 = (bf16[32,32,512]{2,1,0:T(8,128)(2,1)}, bf16[32,32,512]{2,1,0:T(8,128)(2,1)S(1)}, u32[]{:S(2)}, u32[]{:S(2)}) collective-permute-start(bf16[32,32,512]{2,1,0:T(8,128)(2,1)} %get-tuple-element.51), channel_id=1, source_target_pairs={{0,1},{1,0},{2,3},{3,2},{4,5},{5,4},{6,7},{7,6},{8,9},{9,8},{10,11... | collective-permute-start | bytes 3145736 | tf_op jit(solution)/shard_map/ppermute | solution.py:343
  93.9 35.6 %copy-start.1 = (bf16[16,2,32,512]{3,2,1,0:T(8,128)(2,1)S(1)}, bf16[16,2,32,512]{3,2,1,0:T(8,128)(2,1)}, u32[]{:S(2)}) copy-start(bf16[16,2,32,512]{3,2,1,0:T(8,128)(2,1)} %pair_bias.1.bias_ref) | copy-start | bytes 3145732
  93.9 35.6 %copy-start.4 = (bf16[32,128,512]{2,1,0:T(8,128)(2,1)S(1)}, bf16[32,128,512]{2,1,0:T(8,128)(2,1)}, u32[]{:S(2)}) copy-start(bf16[32,128,512]{2,1,0:T(8,128)(2,1)} %get-tuple-element.53.hat_ref) | copy-start | bytes 12582916

commit v5 on v4

--- a/solution.py
+++ b/solution.py
@@ -277,7 +277,7 @@
                 dst[b] = acc_s[position(b, par), :].astype(BF16)
 
 
-def attention(place, mine, other, q, ks, vs, g):
+def attention(place, mine, other, q, ks, vs, masks, g):
     S, dh, I = q.shape
     R, per = len(ks), ks[0].shape[1]
     J = R * per
@@ -285,7 +285,7 @@
     full = lambda a: pl.BlockSpec(a.shape, lambda s: (0,) * a.ndim)
     one = pl.BlockSpec((1, dh, I), lambda s: (s, 0, 0))
     own = pl.BlockSpec((dh, per), lambda s: (s, 0))
-    flags = pl.BlockSpec((MASK, per), lambda s: (S * dh // MASK, 0))
+    flags = pl.BlockSpec((MASK, per), lambda s: (0, 0))
     return pl.pallas_call(
         functools.partial(attend_kernel, R),
         grid=(S,),
@@ -303,23 +303,7 @@
         input_output_aliases={1: 2, 2: 3},
         cost_estimate=pl.CostEstimate(flops=8 * S * J * I * dh, bytes_accessed=12 << 20, transcendentals=S * I * J),
         name="attend",
-    )(place, mine, other, q, g, *ks, *vs, *vs)
-
-
-def pack_kernel(v_ref, m_ref, out_ref):
-    S, dh, per = v_ref.shape
-    out_ref[:S * dh] = v_ref[...].reshape(S * dh, per)
-    out_ref[S * dh:] = jnp.broadcast_to(m_ref[...].astype(F32), (MASK, per)).astype(BF16)
-
-
-def pack(v, mask):
-    S, dh, per = v.shape
-    return pl.pallas_call(
-        pack_kernel,
-        out_shape=jax.ShapeDtypeStruct((S * dh + MASK, per), BF16),
-        compiler_params=pltpu.CompilerParams(vmem_limit_bytes=VMEM),
-        name="pack",
-    )(v, mask.reshape(1, per))
+    )(place, mine, other, q, g, *ks, *vs, *masks)
 
 
 def weight_kernel(weight_ref, gain_ref, out_ref):
@@ -346,16 +330,20 @@
     rows = lax.axis_size("row")
     pass_on = lambda x, n: lax.ppermute(x, "row", [(i, (i + n) % rows) for i in range(rows)])
     k = keys.reshape(-1, strip)
-    v = pack(values[:, 0], key_mask)
+    v = values.reshape(-1, strip)
     k_behind, v_ahead = pass_on(k, 1), pass_on(v, -1)
-    k_ahead, v_behind = pass_on(k, -1), pass_on(v, 1)
+    bias = pair_bias(pair, pair_gain, pair_weight, lax.axis_size("zhi"))
+    bias, k_later, v_later = lax.optimization_barrier((bias, k, v))
+    k_ahead, v_behind = pass_on(k_later, -1), pass_on(v_later, 1)
     k_behind, v_ahead, again = lax.optimization_barrier((k_behind, v_ahead, pair))
     hat, inv = pair_hat(again)
-    k_behind, v_ahead, hat, inv = lax.optimization_barrier((k_behind, v_ahead, hat, inv))
+    flags = jnp.broadcast_to(key_mask.astype(BF16), (MASK, strip))
+    k_behind, v_ahead, hat, inv, flags = lax.optimization_barrier((k_behind, v_ahead, hat, inv, flags))
     ks = [k, k_ahead, pass_on(k_behind, 1), k_behind]
     vs = [v, v_ahead, pass_on(v_ahead, -1), v_behind]
-
-    bias = pair_bias(pair, pair_gain, pair_weight, lax.axis_size("zhi"))
+    masks = [flags, pass_on(flags, -1), pass_on(flags, -2), pass_on(flags, 1)]
+    place = jnp.stack([lax.axis_index("core"), lax.axis_index("row")]).astype(jnp.int32)
+
     heads, copies, width, _ = bias.shape
     mine = spread_out(bias.reshape(heads * copies, width, strip))
 
@@ -367,11 +355,10 @@
         "sda,at->sdt", d_atoms[:, 0], onehot, preferred_element_type=F32
     ).astype(BF16)
     weight = grad_weight(pair_weight, pair_gain)
-    mine, ks, vs, grad_out, weight, hat, inv = lax.optimization_barrier(
-        (mine, ks, vs, grad_out, weight, hat, inv))
+    mine, ks, vs, masks, place, grad_out, weight, hat, inv = lax.optimization_barrier(
+        (mine, ks, vs, masks, place, grad_out, weight, hat, inv))
     other = swap(mine)
-    place = jnp.stack([lax.axis_index("core"), lax.axis_index("row")]).astype(jnp.int32)
-    o, dq, keep, send = attention(place, mine, other, queries[:, 0], ks, vs, grad_out)
+    o, dq, keep, send = attention(place, mine, other, queries[:, 0], ks, vs, masks, grad_out)
 
     chip = (keep.astype(F32) + swap(send).astype(F32)).astype(BF16)
     d_pair = pair_grad(spread_out(chip), bias, inv, hat, weight)

time: 135 us -> 134 us (level)
  waiting for transfers between devices: 19.3 us -> 12.9 us
  starting transfers between devices: 21.8 us -> 24.5 us
  blocking collectives: 33.8 us -> 36.4 us
  Pallas kernels: 54.1 us -> 52.1 us
    all_to_all x1, waiting for transfers between devices: 7.15 us -> 1.56 us  [local(): spread_out = lambda x: lax.all_to_all(x, ('col', 'zhi'), 0, 0, tiled=True)]
    all_to_all x1, blocking collectives: 33.8 us -> 36.4 us  [local(): spread_out = lambda x: lax.all_to_all(x, ('col', 'zhi'), 0, 0, tiled=True)]
    ppermute x6 -> x9, starting transfers between devices: 9.86 us -> 12.3 us  [local(): lax.ppermute(x, 'row', [(i, (i + n) % rows) for i in range(rows)])]
    pallas_call x1 -> x0, Pallas kernels: 1.85 us -> none  [pack(): pl.pallas_call(pack_kernel, out_shape=jax.ShapeDtypeStruct((S * dh + MASK...]
    ppermute x6 -> x9, waiting for transfers between devices: 7.06 us -> 5.75 us  [local(): lax.ppermute(x, 'row', [(i, (i + n) % rows) for i in range(rows)])]
  transfers between devices with their start and end apart: 9 -> 12, of which waited for: 4 -> 4; matrix products, arithmetic and copies ran while one was open for 2% -> 3% of each run, Pallas kernels for 11% -> 10%
where the time goes in v5:
time: 134 us; the launch traced here: 133 us
  Pallas kernels  52.1 us (39%)
  blocking collectives  36.4 us (27%)
  starting transfers between devices  24.5 us (18%)
  waiting for transfers between devices  12.9 us (10%)
  other arithmetic  3.51 us (3%)
  matrix products  2.17 us (2%)
    all_to_all x1, blocking collectives, local(): spread_out = lambda x: lax.all_to_all(x, ('col', 'zhi'), 0, 0, tiled=True)  36.4 us
    pallas_call x1, Pallas kernels, attention(): pl.pallas_call(functools.partial(attend_kernel, R), grid=(S,), in_specs=[...  33.6 us
    ppermute x9, starting transfers between devices, local(): lax.ppermute(x, 'row', [(i, (i + n) % rows) for i in range(rows)])  12.3 us
    all_to_all x1, starting transfers between devices, local(): spread_out = lambda x: lax.all_to_all(x, ('col', 'zhi'), 0, 0, tiled=True)  11.9 us
    pallas_call x1, Pallas kernels, pair_hat(): pl.pallas_call(hat_kernel, grid=(I // block,), in_specs=[pl.BlockSpec((bl...  6.69 us
    pallas_call x1, Pallas kernels, pair_bias(): pl.pallas_call(bias_kernel, grid=(I // block,), in_specs=[pl.BlockSpec((b...  6.52 us
    ppermute x9, waiting for transfers between devices, local(): lax.ppermute(x, 'row', [(i, (i + n) % rows) for i in range(rows)])  5.75 us
    ppermute x2, waiting for transfers between devices, local(): swap = lambda x: lax.ppermute(x, 'core', [(0, 1), (1, 0)])  5.6 us
  transfers between devices with their start and end apart: 12, of which 4 were waited for; matrix products, arithmetic and copies ran while one was open for 3% of the time, Pallas kernels for 10%

profile of v5, /device:TPU:8, one launch (start us, length us, event | category | flops | bytes accessed | tf_op | source)
XLA Modules:
  0.0 133.4 jit_solution(2171780092235273006)
XLA Ops:
  0.6 0.0 copy-start
  0.6 1.6 %collective-permute-start.1 = (bf16[480,512]{1,0:T(8,128)(2,1)}, bf16[480,512]{1,0:T(8,128)(2,1)S(1)}, u32[]{:S(2)}, u32[]{:S(2)}) collective-permute-start(bf16[480,512]{1,0:T(8,128)(2,1)} %bitcast.2.refs_0_), channel_id=1, source_target_pairs={{0,64},{64,128},{128,192},{192,0},{1,65},{65,129},{129,193},{193,1... | collective-permute-start | bytes 1474568 | tf_op jit(solution)/shard_map/ppermute | solution.py:331
  2.2 1.7 %collective-permute-start.2 = (bf16[480,512]{1,0:T(8,128)(2,1)}, bf16[480,512]{1,0:T(8,128)(2,1)S(1)}, u32[]{:S(2)}, u32[]{:S(2)}) collective-permute-start(bf16[480,512]{1,0:T(8,128)(2,1)} %bitcast.3.refs_4_), channel_id=1, source_target_pairs={{0,192},{64,0},{128,64},{192,128},{1,193},{65,1},{129,65},{193,129... | collective-permute-start | bytes 1474568 | tf_op jit(solution)/shard_map/ppermute | solution.py:331
  4.0 6.5 %pair_bias.1.bias_ref = bf16[16,2,32,512]{3,2,1,0:T(8,128)(2,1)} custom-call(bf16[512,32,128]{2,1,0:T(8,128)(2,1)} %pair_ref.2, f32[1,128]{1,0:T(1,128)} %bitcast.33, bf16[16,128]{1,0:T(8,128)(2,1)} %bitcast.31), custom_call_target="tpu_custom_call" | custom-call | flops 107374182400 | bytes 41943040 | tf_op jit(solution)/shard_map/pair_bias/pallas_call | solution.py:66
  10.5 0.0 copy-start.10
  10.5 11.9 %all-to-all-start = ((bf16[32,32,512]{2,1,0:T(8,128)(2,1)}), bf16[32,32,512]{2,1,0:T(8,128)(2,1)}, u32[]{:S(2)}, u32[]{:S(2)}) async-start(bf16[32,32,512]{2,1,0:T(8,128)(2,1)} %bitcast.30), calls=%async_computation | async-start | bytes 2097152 | tf_op jit(solution)/shard_map/all_to_all | solution.py:328
  22.4 1.6 %collective-permute-start = (bf16[480,512]{1,0:T(8,128)(2,1)}, bf16[480,512]{1,0:T(8,128)(2,1)}, u32[]{:S(2)}, u32[]{:S(2)}) collective-permute-start(bf16[480,512]{1,0:T(8,128)(2,1)} %bitcast.2.refs_0_), channel_id=1, source_target_pairs={{0,192},{64,0},{128,64},{192,128},{1,193},{65,1},{129,65},{193,129... | collective-permute-start | bytes 1474568 | tf_op jit(solution)/shard_map/ppermute | solution.py:331
  24.0 0.5 collective-permute-start.5
  24.5 0.0 copy-done.10
  24.5 0.6 convert_element_type.19
  25.1 0.0 copy-done.7
  25.1 0.6 broadcast_subtract_fusion
  25.7 0.0 collective-permute-done.1.refs_3_
  25.7 0.0 collective-permute-done.2.refs_5_
  25.7 0.0 copy-start.13
  25.7 0.0 copy-start.9
  25.7 0.0 copy-start.8
  25.7 6.7 %pair_hat.1 = (bf16[32,128,512]{2,1,0:T(8,128)(2,1)}, f32[32,512]{1,0:T(8,128)}) custom-call(bf16[512,32,128]{2,1,0:T(8,128)(2,1)} %pair_ref.2), custom_call_target="tpu_custom_call" | custom-call | flops 429496729600 | bytes 20971520 | tf_op jit(solution)/shard_map/pair_hat/pallas_call | solution.py:89
  32.4 0.0 copy-done.12
  32.4 0.0 copy-done.13
  32.4 0.0 copy-done.9
  32.4 0.0 copy-start.6
  32.4 0.0 copy-start.2
  32.5 0.0 copy-start.3
  32.5 0.4 collective-permute-start.3
  32.8 3.0 %collective-permute-start.4 = (bf16[480,512]{1,0:T(8,128)(2,1)}, bf16[480,512]{1,0:T(8,128)(2,1)}, u32[]{:S(2)}, u32[]{:S(2)}) collective-permute-start(bf16[480,512]{1,0:T(8,128)(2,1)} %copy-done.13), channel_id=1, source_target_pairs={{0,192},{64,0},{128,64},{192,128},{1,193},{65,1},{129,65},{193,129... | collective-permute-start | bytes 1474568 | tf_op jit(solution)/shard_map/ppermute | solution.py:331
  35.8 0.0 copy-done
  35.8 0.0 copy-done.8
  35.8 2.2 %fusion.10.g_ref = bf16[10,48,512]{2,1,0:T(8,128)(2,1)} fusion(bf16[10,1,48,2048]{3,2,1,0:T(8,128)(2,1)S(1)} %copy-done, s32[2048]{0:T(1024)S(1)} %copy-done.8), kind=kOutput, calls=%fused_computation.7 | convolution fusion | flops 1007927296 | bytes 2465792 | tf_op jit(solution)/shard_map/sda,at->sdt/dot_general | solution.py:354
  38.0 0.0 collective-permute-start.8
  38.0 0.0 collective-permute-done.refs_1_
  38.0 3.0 %collective-permute-start.7 = (bf16[16,512]{1,0:T(8,128)(2,1)S(1)}, bf16[16,512]{1,0:T(8,128)(2,1)S(1)}, u32[]{:S(2)}, u32[]{:S(2)}) collective-permute-start(bf16[16,512]{1,0:T(8,128)(2,1)S(1)} %broadcast_in_dim.11.refs_8_), channel_id=1, source_target_pairs={{0,128},{64,192},{128,0},{192,64},{1,129},{65,193},{129,1},{193,65... | collective-permute-start | bytes 49160 | tf_op jit(solution)/shard_map/ppermute | solution.py:331
  41.0 0.0 collective-permute-done.5.refs_7_
  41.0 0.0 copy-done.6
  41.0 0.6 collective-permute-start.6
  41.6 0.6 pad_add_fusion.place_ref
  42.2 0.0 copy-done.2
  42.2 0.0 copy-done.3
  42.2 0.3 grad_weight.1.weight_ref
  42.5 5.7 %collective-permute-done.8.refs_11_ = bf16[16,512]{1,0:T(8,128)(2,1)S(1)} collective-permute-done((bf16[16,512]{1,0:T(8,128)(2,1)S(1)}, bf16[16,512]{1,0:T(8,128)(2,1)S(1)}, u32[]{:S(2)}, u32[]{:S(2)}) %collective-permute-start.8) | collective-permute-done | bytes 16416 | tf_op jit(solution)/shard_map/ppermute | solution.py:331
  48.2 0.0 collective-permute-done.7.refs_10_
  48.2 0.0 collective-permute-done.6.refs_9_
  48.2 0.0 copy-start.17
  48.3 0.0 collective-permute-done.3.refs_2_
  48.3 0.0 copy-start.14
  48.3 0.0 collective-permute-done.4.refs_6_
  48.3 1.6 %all-to-all-done.mine_ref = bf16[32,32,512]{2,1,0:T(8,128)(2,1)} async-done(((bf16[32,32,512]{2,1,0:T(8,128)(2,1)}), bf16[32,32,512]{2,1,0:T(8,128)(2,1)}, u32[]{:S(2)}, u32[]{:S(2)}) %all-to-all-start) | async-done | bytes 1048608 | tf_op jit(solution)/shard_map/all_to_all | solution.py:328
  49.8 0.0 collective-permute-start.9
  49.9 2.9 %collective-permute-done.9.other_ref = bf16[32,32,512]{2,1,0:T(8,128)(2,1)S(1)} collective-permute-done((bf16[32,32,512]{2,1,0:T(8,128)(2,1)}, bf16[32,32,512]{2,1,0:T(8,128)(2,1)S(1)}, u32[]{:S(2)}, u32[]{:S(2)}) %collective-permute-start.9) | collective-permute-done | bytes 1048608 | tf_op jit(solution)/shard_map/ppermute | solution.py:327
  52.7 1.0 copy-done.11
  53.7 0.0 copy-done.15
  53.7 0.0 copy-done.16
  53.7 0.0 copy-done.17
  53.7 0.0 copy-done.14
  53.7 0.0 copy-start.5
  53.7 33.6 %attend.1 = (bf16[10,48,512]{2,1,0:T(8,128)(2,1)}, bf16[10,48,512]{2,1,0:T(8,128)(2,1)}, bf16[32,32,512]{2,1,0:T(8,128)(2,1)}, bf16[32,32,512]{2,1,0:T(8,128)(2,1)}) custom-call(s32[2]{0:T(128)} %pad_add_fusion.place_ref, bf16[32,32,512]{2,1,0:T(8,128)(2,1)} %all-to-all-done.mine_ref, ...), custom_call_target="tpu_custom_call", output_to_operand_aliasing={{2}: (1, {}), {3}: (2, {})} | custom-call | flops 4026531840 | bytes 12582912 | tf_op jit(solution)/shard_map/attend/pallas_call | solution.py:289
  87.4 0.2 collective-permute-start.10
  87.6 2.7 %collective-permute-done.10 = bf16[32,32,512]{2,1,0:T(8,128)(2,1)S(1)} collective-permute-done((bf16[32,32,512]{2,1,0:T(8,128)(2,1)}, bf16[32,32,512]{2,1,0:T(8,128)(2,1)S(1)}, u32[]{:S(2)}, u32[]{:S(2)}) %collective-permute-start.10) | collective-permute-done | bytes 1048608 | tf_op jit(solution)/shard_map/ppermute | solution.py:327
  90.3 1.7 %add_convert_fusion = bf16[32,32,512]{2,1,0:T(8,128)(2,1)S(1)} fusion(bf16[32,32,512]{2,1,0:T(8,128)(2,1)S(1)} %collective-permute-done.10, bf16[32,32,512]{2,1,0:T(8,128)(2,1)} %get-tuple-element.68), kind=kLoop, calls=%fused_computation.3 | loop fusion | flops 2097152 | bytes 3145728 | tf_op jit(solution)/shard_map/convert_element_type | solution.py:363
  92.1 36.4 %all_to_all.10.part_ref = bf16[32,32,512]{2,1,0:T(8,128)(2,1)S(1)} all-to-all(bf16[32,32,512]{2,1,0:T(8,128)(2,1)S(1)} %add_convert_fusion), channel_id=1, replica_groups=mesh['row'=4,'col'=16,'zhi'=2,'core'=2] {'col','zhi'}, dimensions={0} | all-to-all | bytes 2097152 | tf_op jit(solution)/shard_map/all_to_all | solution.py:328
  128.4 0.0 copy-done.5
  128.4 0.0 copy-done.1
  128.4 0.0 copy-done.4
  128.4 5.0 %pair_grad.1 = bf16[512,32,128]{2,1,0:T(8,128)(2,1)} custom-call(bf16[32,32,512]{2,1,0:T(8,128)(2,1)S(1)} %all_to_all.10.part_ref, bf16[16,2,32,512]{3,2,1,0:T(8,128)(2,1)S(1)} %copy-done.1, f32[32,512]{1,0:T(8,128)S(1)} %copy-done.5, bf16[32,128,512]{2,1,0:T(8,128)(2,1)S(1)} %copy-done.4, bf16[1024,384]{1,0:T(8,128)(2,1)S(1)} %grad_weight.1.weight_ref), custom_call_target="tpu_custom_call" | custom-call | flops 10737418240 | bytes 20971520 | tf_op jit(solution)/shard_map/pair_grad/pallas_call | solution.py:128
  (8 shorter events, 0.0 us)
Async XLA Ops:
  0.6 35.2 %copy-start = (bf16[10,1,48,2048]{3,2,1,0:T(8,128)(2,1)S(1)}, bf16[10,1,48,2048]{3,2,1,0:T(8,128)(2,1)}, u32[]{:S(2)}) copy-start(bf16[10,1,48,2048]{3,2,1,0:T(8,128)(2,1)} %param.15) | copy-start | bytes 5898244
  0.6 25.0 %collective-permute-start.1 = (bf16[480,512]{1,0:T(8,128)(2,1)}, bf16[480,512]{1,0:T(8,128)(2,1)S(1)}, u32[]{:S(2)}, u32[]{:S(2)}) collective-permute-start(bf16[480,512]{1,0:T(8,128)(2,1)} %bitcast.2.refs_0_), channel_id=1, source_target_pairs={{0,64},{64,128},{128,192},{192,0},{1,65},{65,129},{129,193},{193,1... | collective-permute-start | bytes 1474568 | tf_op jit(solution)/shard_map/ppermute | solution.py:331
  2.2 23.5 %collective-permute-start.2 = (bf16[480,512]{1,0:T(8,128)(2,1)}, bf16[480,512]{1,0:T(8,128)(2,1)S(1)}, u32[]{:S(2)}, u32[]{:S(2)}) collective-permute-start(bf16[480,512]{1,0:T(8,128)(2,1)} %bitcast.3.refs_4_), channel_id=1, source_target_pairs={{0,192},{64,0},{128,64},{192,128},{1,193},{65,1},{129,65},{193,129... | collective-permute-start | bytes 1474568 | tf_op jit(solution)/shard_map/ppermute | solution.py:331
  10.5 14.0 %copy-start.10 = (s32[512]{0:T(512)S(1)}, s32[512]{0:T(512)}, u32[]{:S(2)}) copy-start(s32[512]{0:T(512)} %param.16) | copy-start | bytes 6148
  10.5 14.6 %copy-start.7 = (s32[2048]{0:T(1024)S(1)}, s32[2048]{0:T(1024)}, u32[]{:S(2)}) copy-start(s32[2048]{0:T(1024)} %param.17) | copy-start | bytes 24580
  10.5 39.4 %all-to-all-start = ((bf16[32,32,512]{2,1,0:T(8,128)(2,1)}), bf16[32,32,512]{2,1,0:T(8,128)(2,1)}, u32[]{:S(2)}, u32[]{:S(2)}) async-start(bf16[32,32,512]{2,1,0:T(8,128)(2,1)} %bitcast.30), calls=%async_computation | async-start | bytes 2097152 | tf_op jit(solution)/shard_map/all_to_all | solution.py:328
  22.4 15.6 %collective-permute-start = (bf16[480,512]{1,0:T(8,128)(2,1)}, bf16[480,512]{1,0:T(8,128)(2,1)}, u32[]{:S(2)}, u32[]{:S(2)}) collective-permute-start(bf16[480,512]{1,0:T(8,128)(2,1)} %bitcast.2.refs_0_), channel_id=1, source_target_pairs={{0,192},{64,0},{128,64},{192,128},{1,193},{65,1},{129,65},{193,129... | collective-permute-start | bytes 1474568 | tf_op jit(solution)/shard_map/ppermute | solution.py:331
  24.0 17.0 %collective-permute-start.5 = (bf16[480,512]{1,0:T(8,128)(2,1)}, bf16[480,512]{1,0:T(8,128)(2,1)}, u32[]{:S(2)}, u32[]{:S(2)}) collective-permute-start(bf16[480,512]{1,0:T(8,128)(2,1)} %bitcast.3.refs_4_), channel_id=1, source_target_pairs={{0,64},{64,128},{128,192},{192,0},{1,65},{65,129},{129,193},{193,1... | collective-permute-start | bytes 1474568 | tf_op jit(solution)/shard_map/ppermute | solution.py:331
  25.7 6.7 %copy-start.12 = (bf16[480,512]{1,0:T(8,128)(2,1)}, bf16[480,512]{1,0:T(8,128)(2,1)S(1)}, u32[]{:S(2)}) copy-start(bf16[480,512]{1,0:T(8,128)(2,1)S(1)} %collective-permute-done.1.refs_3_) | copy-start | bytes 1474564
  25.7 6.7 %copy-start.13 = (bf16[480,512]{1,0:T(8,128)(2,1)}, bf16[480,512]{1,0:T(8,128)(2,1)S(1)}, u32[]{:S(2)}) copy-start(bf16[480,512]{1,0:T(8,128)(2,1)S(1)} %collective-permute-done.2.refs_5_) | copy-start | bytes 1474564
  25.7 6.7 %copy-start.9 = (bf16[512]{0:T(512)(128)(2,1)S(1)}, bf16[512]{0:T(512)(128)(2,1)}, u32[]{:S(2)}) copy-start(bf16[512]{0:T(512)(128)(2,1)} %convert_element_type.19) | copy-start | bytes 3076
  25.7 10.1 %copy-start.8 = (s32[2048]{0:T(1024)S(1)}, s32[2048]{0:T(1024)}, u32[]{:S(2)}) copy-start(s32[2048]{0:T(1024)} %broadcast_subtract_fusion) | copy-start | bytes 24580
  32.4 8.5 %copy-start.6 = (bf16[16,512]{1,0:T(8,128)(2,1)}, bf16[16,512]{1,0:T(8,128)(2,1)S(1)}, u32[]{:S(2)}) copy-start(bf16[16,512]{1,0:T(8,128)(2,1)S(1)} %broadcast_in_dim.11.refs_8_) | copy-start | bytes 49156
  32.4 9.7 %copy-start.2 = (bf16[128,16]{0,1:T(8,128)(2,1)S(1)}, bf16[128,16]{0,1:T(8,128)(2,1)}, u32[]{:S(2)}) copy-start(bf16[128,16]{0,1:T(8,128)(2,1)} %param.11) | copy-start | bytes 12292
  32.5 9.7 %copy-start.3 = (f32[128]{0:T(128)S(1)}, f32[128]{0:T(128)}, u32[]{:S(2)}) copy-start(f32[128]{0:T(128)} %param.10) | copy-start | bytes 1540
  32.5 15.8 %collective-permute-start.3 = (bf16[480,512]{1,0:T(8,128)(2,1)}, bf16[480,512]{1,0:T(8,128)(2,1)S(1)}, u32[]{:S(2)}, u32[]{:S(2)}) collective-permute-start(bf16[480,512]{1,0:T(8,128)(2,1)} %copy-done.12), channel_id=1, source_target_pairs={{0,64},{64,128},{128,192},{192,0},{1,65},{65,129},{129,193},{193,1... | collective-permute-start | bytes 1474568 | tf_op jit(solution)/shard_map/ppermute | solution.py:331
  32.8 15.5 %collective-permute-start.4 = (bf16[480,512]{1,0:T(8,128)(2,1)}, bf16[480,512]{1,0:T(8,128)(2,1)}, u32[]{:S(2)}, u32[]{:S(2)}) collective-permute-start(bf16[480,512]{1,0:T(8,128)(2,1)} %copy-done.13), channel_id=1, source_target_pairs={{0,192},{64,0},{128,64},{192,128},{1,193},{65,1},{129,65},{193,129... | collective-permute-start | bytes 1474568 | tf_op jit(solution)/shard_map/ppermute | solution.py:331
  38.0 10.3 %collective-permute-start.8 = (bf16[16,512]{1,0:T(8,128)(2,1)S(1)}, bf16[16,512]{1,0:T(8,128)(2,1)S(1)}, u32[]{:S(2)}, u32[]{:S(2)}) collective-permute-start(bf16[16,512]{1,0:T(8,128)(2,1)S(1)} %broadcast_in_dim.11.refs_8_), channel_id=1, source_target_pairs={{0,64},{64,128},{128,192},{192,0},{1,65},{65,129},{129,193},{193,1... | collective-permute-start | bytes 49160 | tf_op jit(solution)/shard_map/ppermute | solution.py:331
  38.0 10.3 %collective-permute-start.7 = (bf16[16,512]{1,0:T(8,128)(2,1)S(1)}, bf16[16,512]{1,0:T(8,128)(2,1)S(1)}, u32[]{:S(2)}, u32[]{:S(2)}) collective-permute-start(bf16[16,512]{1,0:T(8,128)(2,1)S(1)} %broadcast_in_dim.11.refs_8_), channel_id=1, source_target_pairs={{0,128},{64,192},{128,0},{192,64},{1,129},{65,193},{129,1},{193,65... | collective-permute-start | bytes 49160 | tf_op jit(solution)/shard_map/ppermute | solution.py:331
  41.0 7.3 %collective-permute-start.6 = (bf16[16,512]{1,0:T(8,128)(2,1)S(1)}, bf16[16,512]{1,0:T(8,128)(2,1)S(1)}, u32[]{:S(2)}, u32[]{:S(2)}) collective-permute-start(bf16[16,512]{1,0:T(8,128)(2,1)S(1)} %broadcast_in_dim.11.refs_8_), channel_id=1, source_target_pairs={{0,192},{64,0},{128,64},{192,128},{1,193},{65,1},{129,65},{193,129... | collective-permute-start | bytes 49160 | tf_op jit(solution)/shard_map/ppermute | solution.py:331
  48.2 5.5 %copy-start.15 = (bf16[16,512]{1,0:T(8,128)(2,1)}, bf16[16,512]{1,0:T(8,128)(2,1)S(1)}, u32[]{:S(2)}) copy-start(bf16[16,512]{1,0:T(8,128)(2,1)S(1)} %collective-permute-done.8.refs_11_) | copy-start | bytes 49156
  48.2 5.5 %copy-start.16 = (bf16[16,512]{1,0:T(8,128)(2,1)}, bf16[16,512]{1,0:T(8,128)(2,1)S(1)}, u32[]{:S(2)}) copy-start(bf16[16,512]{1,0:T(8,128)(2,1)S(1)} %collective-permute-done.7.refs_10_) | copy-start | bytes 49156
  48.2 5.5 %copy-start.17 = (bf16[16,512]{1,0:T(8,128)(2,1)}, bf16[16,512]{1,0:T(8,128)(2,1)S(1)}, u32[]{:S(2)}) copy-start(bf16[16,512]{1,0:T(8,128)(2,1)S(1)} %collective-permute-done.6.refs_9_) | copy-start | bytes 49156
  48.3 5.5 %copy-start.14 = (bf16[480,512]{1,0:T(8,128)(2,1)}, bf16[480,512]{1,0:T(8,128)(2,1)S(1)}, u32[]{:S(2)}) copy-start(bf16[480,512]{1,0:T(8,128)(2,1)S(1)} %collective-permute-done.3.refs_2_) | copy-start | bytes 1474564
  49.8 2.9 %collective-permute-start.9 = (bf16[32,32,512]{2,1,0:T(8,128)(2,1)}, bf16[32,32,512]{2,1,0:T(8,128)(2,1)S(1)}, u32[]{:S(2)}, u32[]{:S(2)}) collective-permute-start(bf16[32,32,512]{2,1,0:T(8,128)(2,1)} %all-to-all-done.mine_ref), channel_id=1, source_target_pairs={{0,1},{1,0},{2,3},{3,2},{4,5},{5,4},{6,7},{7,6},{8,9},{9,8},{10,11... | collective-permute-start | bytes 3145736 | tf_op jit(solution)/shard_map/ppermute | solution.py:327
  52.7 1.0 copy-start.11
  53.7 74.7 %copy-start.5 = (f32[32,512]{1,0:T(8,128)S(1)}, f32[32,512]{1,0:T(8,128)}, u32[]{:S(2)}) copy-start(f32[32,512]{1,0:T(8,128)} %get-tuple-element.70.inv_ref) | copy-start | bytes 196612
  87.4 3.0 %collective-permute-start.10 = (bf16[32,32,512]{2,1,0:T(8,128)(2,1)}, bf16[32,32,512]{2,1,0:T(8,128)(2,1)S(1)}, u32[]{:S(2)}, u32[]{:S(2)}) collective-permute-start(bf16[32,32,512]{2,1,0:T(8,128)(2,1)} %get-tuple-element.69), channel_id=1, source_target_pairs={{0,1},{1,0},{2,3},{3,2},{4,5},{5,4},{6,7},{7,6},{8,9},{9,8},{10,11... | collective-permute-start | bytes 3145736 | tf_op jit(solution)/shard_map/ppermute | solution.py:327
  90.3 38.1 %copy-start.1 = (bf16[16,2,32,512]{3,2,1,0:T(8,128)(2,1)S(1)}, bf16[16,2,32,512]{3,2,1,0:T(8,128)(2,1)}, u32[]{:S(2)}) copy-start(bf16[16,2,32,512]{3,2,1,0:T(8,128)(2,1)} %pair_bias.1.bias_ref) | copy-start | bytes 3145732
  90.3 38.1 %copy-start.4 = (bf16[32,128,512]{2,1,0:T(8,128)(2,1)S(1)}, bf16[32,128,512]{2,1,0:T(8,128)(2,1)}, u32[]{:S(2)}) copy-start(bf16[32,128,512]{2,1,0:T(8,128)(2,1)} %get-tuple-element.71.hat_ref) | copy-start | bytes 12582916
